TPU v7x, 32 devices: a whole 2x2x4 slice. The times are simulated.
32 devices in a mesh: ctx: 4 (over y, x), mp: 8 (over z, core).
Axes of the slice: x: 2, y: 2, z: 4, core: 2. Of those that a mesh axis runs over, the one named last changes fastest.
Arguments:
- residual_in: bfloat16 [2048, 8192], P('ctx', 'mp'), may hold values from -4 to 4
- query_rows: bfloat16 [2048, 8192], P('ctx', 'mp'), may hold values from -5 to 5
- key_rows: bfloat16 [2048, 8192], P('ctx', 'mp'), may hold values from -5 to 5
- value_rows: bfloat16 [2048, 8192], P('ctx', 'mp'), may hold values from -5 to 5
- out_weight: bfloat16 [8192, 8192], P('mp'), may hold values from -0.75 to 0.75
- gate_in: bfloat16 [2048, 8192], P('ctx', 'mp'), may hold values from -5 to 5
- gate_out: bfloat16 [2048, 8192], P('ctx', 'mp'), may hold values from -5 to 5
- short_taps: float32 [3, 8192], P(None, 'mp'), may hold values from -3 to 3
- decay_rates: float32 [16, 8192], P(None, 'mp'), may hold values from 9.765625e-05 to 0.03
- residues: float32 [16, 8192], P(None, 'mp'), may hold values from -0.15 to 0.15
- skip_gain: float32 [8192], P('mp'), may hold values from -4 to 4
Outputs:
- attended: bfloat16 [2048, 8192], P('ctx', 'mp')
- hyena_out: bfloat16 [2048, 8192], P('ctx', 'mp')
All inputs are finite; a program needn't handle non-finite values.
Results may differ from a plain program's by a relative error of at most 0.02.
Values may be sent and summed in bfloat16 or wider, within the bound.
A program may use at most 128 MiB of HBM per device.

v0:
```python
import jax
import jax.numpy as jnp
from jax import lax
from jax.sharding import PartitionSpec as P

HD = 128
BLOCK = 64


masked_floor = -1e30


def from_behind(value, axis, steps):
    count = lax.axis_size(axis)
    leading, last = (max(0, -steps), min(count, count - steps))
    return lax.ppermute(value, axis, [(source, source + steps) for source in range(leading, last)])


def modal_tables(decay_rates, residues, block):
    width = decay_rates.shape[1]
    lags = jnp.arange(block).astype(jnp.float32)
    lag_diff = lags[:, None] - lags[None, :]
    causal = lag_diff >= 0
    safe_diff = jnp.maximum(lag_diff, 0.0)

    def add_pole(total, pole):
        rate, residue = pole
        return (
            total + residue[None, None, :] * jnp.exp(-rate[None, None, :] * safe_diff[:, :, None]),
            None,
        )

    toeplitz, _ = lax.scan(
        add_pole, jnp.zeros((block, block, width), jnp.float32), (decay_rates, residues)
    )
    toeplitz = jnp.where(causal[:, :, None], toeplitz, 0.0)
    powers = jnp.exp(-decay_rates[None] * lags[:, None, None])
    inward = jnp.exp(-decay_rates[None] * (block - lags)[:, None, None])
    return (toeplitz, powers, inward)


def modal_conv(signal, decay_rates, residues, block):
    length, width = signal.shape
    toeplitz, powers, inward = modal_tables(decay_rates, residues, block)
    highest = lax.Precision.HIGHEST
    span = jnp.exp(-decay_rates * block)

    def modal_step(state, piece):
        local = jnp.einsum("ijc,jc->ic", toeplitz, piece, precision=highest)
        carried = jnp.einsum("inc,nc->ic", powers, residues * state, precision=highest)
        state = span * state + jnp.einsum("jnc,jc->nc", inward, piece, precision=highest)
        return (state, local + carried)

    start_state = jnp.zeros((decay_rates.shape[0], width), jnp.float32)
    state, result = lax.scan(modal_step, start_state, signal.reshape(length // block, block, width))
    return (result.reshape(length, width), state)


def attend(groups, key_rows, value_rows):
    width = key_rows.shape[1]
    heads = width // HD
    scale = HD ** (-0.5)
    query_sets = [(rows_q.reshape(rows_q.shape[0], heads, HD), pos_q) for rows_q, pos_q in groups]

    def update(state, queries, query_pos, keys_here, values_here, key_pos):
        running_top, running_total, running_sum = state
        scores = (
            jnp.einsum("qhd,khd->hqk", queries, keys_here, preferred_element_type=jnp.float32)
            * scale
        )
        allowed = (key_pos[None, :] <= query_pos[:, None])[None]
        masked = jnp.where(allowed, scores, masked_floor)
        new_top = jnp.maximum(running_top, jnp.max(masked, axis=-1))
        weights = jnp.where(allowed, jnp.exp(masked - new_top[..., None]), 0.0)
        rescale = jnp.exp(running_top - new_top)
        new_total = running_total * rescale + jnp.sum(weights, axis=-1)
        new_sum = running_sum * rescale[..., None] + jnp.einsum(
            "hqk,khd->hqd",
            weights.astype(jnp.bfloat16),
            values_here,
            preferred_element_type=jnp.float32,
        )
        return (new_top, new_total, new_sum)

    initial = tuple(
        (
            (
                jnp.full((heads, pos_q.shape[0]), masked_floor, jnp.float32),
                jnp.zeros((heads, pos_q.shape[0]), jnp.float32),
                jnp.zeros((heads, pos_q.shape[0], HD), jnp.float32),
            )
            for rows_q, pos_q in groups
        )
    )
    pieces = (
        lax.all_gather(key_rows, "ctx", axis=0, tiled=True),
        lax.all_gather(value_rows, "ctx", axis=0, tiled=True),
    )
    count = pieces[0].shape[0]
    blocks = count // count
    keys_all = pieces[0].reshape(blocks, count, heads, HD)
    values_all = pieces[1].reshape(blocks, count, heads, HD)
    index_rows = jnp.arange(count)
    pos_all = index_rows.reshape(blocks, count)

    def fold_step(states, block):
        keys_here, values_here, key_pos = block
        return (
            tuple(
                (
                    update(
                        states[g],
                        query_sets[g][0],
                        query_sets[g][1],
                        keys_here,
                        values_here,
                        key_pos,
                    )
                    for g in range(len(query_sets))
                )
            ),
            None,
        )

    result, _ = lax.scan(fold_step, initial, (keys_all, values_all, pos_all))
    return [(final[2] / final[1][..., None]).astype(jnp.bfloat16) for final in result]


def per_device(
    residual_in,
    query_rows,
    key_rows,
    value_rows,
    out_weight,
    gate_in,
    gate_out,
    short_taps,
    decay_rates,
    residues,
    skip_gain,
):
    rows = residual_in.shape[0]
    width = residual_in.shape[1]
    segment = lax.axis_index("ctx")
    query_pos = segment * rows + jnp.arange(rows)
    heads_out = attend([(query_rows, query_pos)], key_rows, value_rows)[0]
    heads = heads_out.shape[0]
    columns = out_weight.reshape(heads, HD, width * lax.axis_size("mp"))
    projected = lax.psum_scatter(
        jnp.einsum("hqd,hdc->cq", heads_out, columns, preferred_element_type=jnp.float32).astype(
            jnp.bfloat16
        ),
        "mp",
        scatter_dimension=0,
        tiled=True,
    ).astype(jnp.float32)
    attended = (residual_in.astype(jnp.float32) + projected.T).astype(jnp.bfloat16)
    taps = short_taps.shape[0]
    rim = from_behind(attended[rows - (taps - 1) :], "ctx", 1)
    extended = jnp.concatenate([rim, attended], axis=0).astype(jnp.float32)
    shortconv = jnp.zeros((rows, width), jnp.float32)
    for tap in range(taps):
        shortconv = (
            shortconv + short_taps[tap][None, :] * extended[taps - 1 - tap : taps - 1 - tap + rows]
        )
    signal = gate_in.astype(jnp.float32) * shortconv
    local, final_state = modal_conv(signal, decay_rates, residues, BLOCK)
    highest = lax.Precision.HIGHEST
    lag_rows = jnp.arange(rows).astype(jnp.float32)
    long_powers = residues[None] * jnp.exp(-decay_rates[None] * lag_rows[:, None, None])
    piece = lax.all_gather(final_state[None], "ctx", axis=0, tiled=True)
    count = piece.shape[0]
    earlier_index = jnp.arange(count)
    gap = jnp.maximum((segment - earlier_index - 1) * rows, 0).astype(jnp.float32)
    factor = jnp.where(
        (earlier_index < segment)[:, None, None],
        jnp.exp(-decay_rates[None] * gap[:, None, None]),
        0.0,
    )
    state_before = jnp.sum(factor * piece, axis=0)
    carried = jnp.einsum("inc,nc->ic", long_powers, state_before, precision=highest)
    hyena_out = (
        gate_out.astype(jnp.float32) * (local + carried + skip_gain[None, :] * signal)
    ).astype(jnp.bfloat16)
    return (attended, hyena_out)


def solution(mesh):
    in_specs = (
        P("ctx", "mp"),
        P("ctx", "mp"),
        P("ctx", "mp"),
        P("ctx", "mp"),
        P("mp", None),
        P("ctx", "mp"),
        P("ctx", "mp"),
        P(None, "mp"),
        P(None, "mp"),
        P(None, "mp"),
        P("mp"),
    )
    out_specs = (P("ctx", "mp"), P("ctx", "mp"))
    return jax.shard_map(
        per_device, mesh=mesh, in_specs=in_specs, out_specs=out_specs, check_vma=False
    )
```

profile of v0, /device:TPU:0, one launch (start us, length us, event | category | flops | bytes accessed | tf_op | source)
XLA Modules:
  0.0 486.8 jit_solution(17289858804982921347)
XLA Ops:
  11.1 54.6 %all-gather.4.cloned.1.call-done = bf16[2048,1024]{0,1:T(8,128)(2,1)} async-done(((bf16[512,1024]{0,1:T(8,128)(2,1)}), bf16[2048,1024]{0,1:T(8,128)(2,1)}) %all-gather.4.cloned.1.call-update) | async-done | bytes 4194320 | tf_op jit(solution)/shard_map/all_gather | solution.py:96
  65.7 17.4 %fusion.6 = (f32[8,512]{1,0:T(8,128)S(1)}, f32[8,512,2048]{2,1,0:T(8,128)}) fusion(pred[512,2048]{1,0:T(8,128)(4,1)S(1)} %iota_compare_fusion, bf16[2048,8,128]{0,2,1:T(8,128)(2,1)} %bitcast.103, bf16[512,1024]{1,0:T(8,128)(2,1)S(1)} %copy-done), kind=kOutput, calls=%fused_computation.17 | convolution fusion | flops 2172645376 | bytes 39862272 | tf_op jit(solution)/shard_map/while/body/eval_jaxpr/qhd,khd->hqk/dot_general | solution.py:68
  83.1 16.1 %fusion.7 = f32[8,512]{1,0:T(8,128)S(1)} fusion(f32[8,512,2048]{2,1,0:T(8,128)} %get-tuple-element.265, f32[8,512]{1,0:T(8,128)S(1)} %broadcast_maximum_fusion, pred[512,2048]{1,0:T(8,128)(4,1)S(1)} %iota_compare_fusion), kind=kLoop, calls=%fused_computation.18 | loop fusion | flops 41938944 | bytes 34635776 | tf_op jit(solution)/shard_map/while/body/eval_jaxpr/reduce_sum | solution.py:76
  99.2 21.1 %all-gather.6.cloned.1.call-done = bf16[2048,1024]{1,0:T(8,128)(2,1)} async-done(((bf16[512,1024]{1,0:T(8,128)(2,1)}), bf16[2048,1024]{1,0:T(8,128)(2,1)}) %all-gather.6.cloned.1.call-update) | async-done | bytes 4194320 | tf_op jit(solution)/shard_map/all_gather | solution.py:97
  120.3 16.6 %divide_convert_fusion.clone.4 = bf16[8,512,128]{2,1,0:T(8,128)(2,1)S(1)} fusion(f32[8,512,2048]{2,1,0:T(8,128)} %get-tuple-element.265, f32[8,512]{1,0:T(8,128)S(1)} %broadcast_maximum_fusion, pred[512,2048]{1,0:T(8,128)(4,1)S(1)} %iota_compare_fusion, f32[8,512]{1,0:T(8,128)S(1)} %get-tuple-element.263, ...), kind=kOutput, calls=%fused_computation.40.clone.clone.clone.1 | convolution fusion | flops 2190999552 | bytes 39895040 | tf_op jit(solution)/shard_map/while/body/eval_jaxpr/hqk,khd->hqd/dot_general | solution.py:77
  137.0 14.0 %fusion.12 = bf16[8192,512]{0,1:T(8,128)(2,1)} fusion(bf16[8,128,8192]{2,1,0:T(8,128)(2,1)} %bitcast.111, bf16[8,512,128]{2,1,0:T(8,128)(2,1)S(1)} %divide_convert_fusion.clone.4), kind=kOutput, calls=%fused_computation.23 | convolution fusion | flops 8594128896 | bytes 26214400 | tf_op jit(solution)/shard_map/hqd,hdc->cq/dot_general | solution.py:150
  151.8 194.7 %while.32 = (s32[]{:T(128)}, f32[64,64,1024]{2,1,0:T(8,128)}, f32[16,1024]{1,0:T(8,128)S(1)}, f32[16,1024]{1,0:T(8,128)S(1)}, f32[64]{0:T(128)S(1)}, /*index=5*/s32[]{:T(128)}, s32[]{:T(128)}) while((s32[]{:T(128)}, f32[64,64,1024]{2,1,0:T(8,128)}, f32[16,1024]{1,0:T(8,128)S(1)}, f32[16,1024]{1,0:T(8,128)S(1)}, f32[64]{0:T(128)S(1)}, ...), condition=%wide.region_4.5_spmd.clone, body=%wide.region_3.4_spmd.clone.sunk | while | flops 16786436 | bytes 33612120 | solution.py:33
  159.2 12.5 %select_add_fusion.2 = f32[64,64,1024]{2,1,0:T(8,128)} fusion(f32[64,64,1024]{2,1,0:T(8,128)} %get-tuple-element.374, f32[64,64]{1,0:T(8,128)S(1)} %subtract_maximum_fusion.2, f32[1024]{0:T(1024)S(1)} %bitcast.105, f32[1024]{0:T(1024)S(1)} %bitcast.106, pred[]{:T(512)S(6)} %compare.8), kind=kLoop, calls=%fused_computation.3.clone.1 | loop fusion | flops 16777216 | bytes 33579008 | tf_op jit(solution)/shard_map/while/body/eval_jaxpr/add | solution.py:29
  171.7 12.5 %select_add_fusion.2 = f32[64,64,1024]{2,1,0:T(8,128)} fusion(f32[64,64,1024]{2,1,0:T(8,128)} %get-tuple-element.374, f32[64,64]{1,0:T(8,128)S(1)} %subtract_maximum_fusion.2, f32[1024]{0:T(1024)S(1)} %bitcast.105, f32[1024]{0:T(1024)S(1)} %bitcast.106, pred[]{:T(512)S(6)} %compare.8), kind=kLoop, calls=%fused_computation.3.clone.1 | loop fusion | flops 16777216 | bytes 33579008 | tf_op jit(solution)/shard_map/while/body/eval_jaxpr/add | solution.py:29
  184.3 12.5 %select_add_fusion.2 = f32[64,64,1024]{2,1,0:T(8,128)} fusion(f32[64,64,1024]{2,1,0:T(8,128)} %get-tuple-element.374, f32[64,64]{1,0:T(8,128)S(1)} %subtract_maximum_fusion.2, f32[1024]{0:T(1024)S(1)} %bitcast.105, f32[1024]{0:T(1024)S(1)} %bitcast.106, pred[]{:T(512)S(6)} %compare.8), kind=kLoop, calls=%fused_computation.3.clone.1 | loop fusion | flops 16777216 | bytes 33579008 | tf_op jit(solution)/shard_map/while/body/eval_jaxpr/add | solution.py:29
  196.9 12.4 %select_add_fusion.2 = f32[64,64,1024]{2,1,0:T(8,128)} fusion(f32[64,64,1024]{2,1,0:T(8,128)} %get-tuple-element.374, f32[64,64]{1,0:T(8,128)S(1)} %subtract_maximum_fusion.2, f32[1024]{0:T(1024)S(1)} %bitcast.105, f32[1024]{0:T(1024)S(1)} %bitcast.106, pred[]{:T(512)S(6)} %compare.8), kind=kLoop, calls=%fused_computation.3.clone.1 | loop fusion | flops 16777216 | bytes 33579008 | tf_op jit(solution)/shard_map/while/body/eval_jaxpr/add | solution.py:29
  209.4 12.5 %select_add_fusion.2 = f32[64,64,1024]{2,1,0:T(8,128)} fusion(f32[64,64,1024]{2,1,0:T(8,128)} %get-tuple-element.374, f32[64,64]{1,0:T(8,128)S(1)} %subtract_maximum_fusion.2, f32[1024]{0:T(1024)S(1)} %bitcast.105, f32[1024]{0:T(1024)S(1)} %bitcast.106, pred[]{:T(512)S(6)} %compare.8), kind=kLoop, calls=%fused_computation.3.clone.1 | loop fusion | flops 16777216 | bytes 33579008 | tf_op jit(solution)/shard_map/while/body/eval_jaxpr/add | solution.py:29
  222.0 12.4 %select_add_fusion.2 = f32[64,64,1024]{2,1,0:T(8,128)} fusion(f32[64,64,1024]{2,1,0:T(8,128)} %get-tuple-element.374, f32[64,64]{1,0:T(8,128)S(1)} %subtract_maximum_fusion.2, f32[1024]{0:T(1024)S(1)} %bitcast.105, f32[1024]{0:T(1024)S(1)} %bitcast.106, pred[]{:T(512)S(6)} %compare.8), kind=kLoop, calls=%fused_computation.3.clone.1 | loop fusion | flops 16777216 | bytes 33579008 | tf_op jit(solution)/shard_map/while/body/eval_jaxpr/add | solution.py:29
  234.5 12.4 %select_add_fusion.2 = f32[64,64,1024]{2,1,0:T(8,128)} fusion(f32[64,64,1024]{2,1,0:T(8,128)} %get-tuple-element.374, f32[64,64]{1,0:T(8,128)S(1)} %subtract_maximum_fusion.2, f32[1024]{0:T(1024)S(1)} %bitcast.105, f32[1024]{0:T(1024)S(1)} %bitcast.106, pred[]{:T(512)S(6)} %compare.8), kind=kLoop, calls=%fused_computation.3.clone.1 | loop fusion | flops 16777216 | bytes 33579008 | tf_op jit(solution)/shard_map/while/body/eval_jaxpr/add | solution.py:29
  247.0 12.4 %select_add_fusion.2 = f32[64,64,1024]{2,1,0:T(8,128)} fusion(f32[64,64,1024]{2,1,0:T(8,128)} %get-tuple-element.374, f32[64,64]{1,0:T(8,128)S(1)} %subtract_maximum_fusion.2, f32[1024]{0:T(1024)S(1)} %bitcast.105, f32[1024]{0:T(1024)S(1)} %bitcast.106, pred[]{:T(512)S(6)} %compare.8), kind=kLoop, calls=%fused_computation.3.clone.1 | loop fusion | flops 16777216 | bytes 33579008 | tf_op jit(solution)/shard_map/while/body/eval_jaxpr/add | solution.py:29
  259.5 12.4 %select_add_fusion.2 = f32[64,64,1024]{2,1,0:T(8,128)} fusion(f32[64,64,1024]{2,1,0:T(8,128)} %get-tuple-element.374, f32[64,64]{1,0:T(8,128)S(1)} %subtract_maximum_fusion.2, f32[1024]{0:T(1024)S(1)} %bitcast.105, f32[1024]{0:T(1024)S(1)} %bitcast.106, pred[]{:T(512)S(6)} %compare.8), kind=kLoop, calls=%fused_computation.3.clone.1 | loop fusion | flops 16777216 | bytes 33579008 | tf_op jit(solution)/shard_map/while/body/eval_jaxpr/add | solution.py:29
  271.9 12.4 %select_add_fusion.2 = f32[64,64,1024]{2,1,0:T(8,128)} fusion(f32[64,64,1024]{2,1,0:T(8,128)} %get-tuple-element.374, f32[64,64]{1,0:T(8,128)S(1)} %subtract_maximum_fusion.2, f32[1024]{0:T(1024)S(1)} %bitcast.105, f32[1024]{0:T(1024)S(1)} %bitcast.106, pred[]{:T(512)S(6)} %compare.8), kind=kLoop, calls=%fused_computation.3.clone.1 | loop fusion | flops 16777216 | bytes 33579008 | tf_op jit(solution)/shard_map/while/body/eval_jaxpr/add | solution.py:29
  284.3 12.4 %select_add_fusion.2 = f32[64,64,1024]{2,1,0:T(8,128)} fusion(f32[64,64,1024]{2,1,0:T(8,128)} %get-tuple-element.374, f32[64,64]{1,0:T(8,128)S(1)} %subtract_maximum_fusion.2, f32[1024]{0:T(1024)S(1)} %bitcast.105, f32[1024]{0:T(1024)S(1)} %bitcast.106, pred[]{:T(512)S(6)} %compare.8), kind=kLoop, calls=%fused_computation.3.clone.1 | loop fusion | flops 16777216 | bytes 33579008 | tf_op jit(solution)/shard_map/while/body/eval_jaxpr/add | solution.py:29
  296.8 12.4 %select_add_fusion.2 = f32[64,64,1024]{2,1,0:T(8,128)} fusion(f32[64,64,1024]{2,1,0:T(8,128)} %get-tuple-element.374, f32[64,64]{1,0:T(8,128)S(1)} %subtract_maximum_fusion.2, f32[1024]{0:T(1024)S(1)} %bitcast.105, f32[1024]{0:T(1024)S(1)} %bitcast.106, pred[]{:T(512)S(6)} %compare.8), kind=kLoop, calls=%fused_computation.3.clone.1 | loop fusion | flops 16777216 | bytes 33579008 | tf_op jit(solution)/shard_map/while/body/eval_jaxpr/add | solution.py:29
  309.2 12.4 %select_add_fusion.2 = f32[64,64,1024]{2,1,0:T(8,128)} fusion(f32[64,64,1024]{2,1,0:T(8,128)} %get-tuple-element.374, f32[64,64]{1,0:T(8,128)S(1)} %subtract_maximum_fusion.2, f32[1024]{0:T(1024)S(1)} %bitcast.105, f32[1024]{0:T(1024)S(1)} %bitcast.106, pred[]{:T(512)S(6)} %compare.8), kind=kLoop, calls=%fused_computation.3.clone.1 | loop fusion | flops 16777216 | bytes 33579008 | tf_op jit(solution)/shard_map/while/body/eval_jaxpr/add | solution.py:29
  321.7 12.4 %select_add_fusion.2 = f32[64,64,1024]{2,1,0:T(8,128)} fusion(f32[64,64,1024]{2,1,0:T(8,128)} %get-tuple-element.374, f32[64,64]{1,0:T(8,128)S(1)} %subtract_maximum_fusion.2, f32[1024]{0:T(1024)S(1)} %bitcast.105, f32[1024]{0:T(1024)S(1)} %bitcast.106, pred[]{:T(512)S(6)} %compare.8), kind=kLoop, calls=%fused_computation.3.clone.1 | loop fusion | flops 16777216 | bytes 33579008 | tf_op jit(solution)/shard_map/while/body/eval_jaxpr/add | solution.py:29
  334.1 12.4 %select_add_fusion.2 = f32[64,64,1024]{2,1,0:T(8,128)} fusion(f32[64,64,1024]{2,1,0:T(8,128)} %get-tuple-element.374, f32[64,64]{1,0:T(8,128)S(1)} %subtract_maximum_fusion.2, f32[1024]{0:T(1024)S(1)} %bitcast.105, f32[1024]{0:T(1024)S(1)} %bitcast.106, pred[]{:T(512)S(6)} %compare.8), kind=kLoop, calls=%fused_computation.3.clone.1 | loop fusion | flops 16777216 | bytes 33579008 | tf_op jit(solution)/shard_map/while/body/eval_jaxpr/add | solution.py:29
  346.7 11.5 %broadcast_select_fusion = f32[64,64,1024]{2,1,0:T(8,128)} fusion(f32[64,64,1024]{2,1,0:T(8,128)} %get-tuple-element.104, pred[64,64]{1,0:T(8,128)(4,1)S(1)} %subtract_compare_fusion), kind=kLoop, calls=%fused_computation.24 | loop fusion | flops 4194304 | bytes 33558528 | tf_op jit(solution)/shard_map/jit(_where)/select_n | solution.py:36
  366.8 89.9 %while.33 = (s32[]{:T(128)}, f32[16,1024]{1,0:T(8,128)S(1)}, f32[8,64,1024]{2,1,0:T(8,128)}, f32[16,1024]{1,0:T(8,128)S(1)}, f32[8,64,1024]{2,1,0:T(8,128)S(1)},...) while((s32[]{:T(128)}, f32[16,1024]{1,0:T(8,128)S(1)}, ...), condition=%wide.region_6.7_spmd.clone.clone.clone, body=%wide.region_5.6_spmd.clone.clone.clone.sunk | while | flops 14663683 | bytes 19793028 | solution.py:55
  368.9 8.4 %multiply_reduce_fusion.9 = f32[1024,64]{0,1:T(8,128)S(1)} fusion(f32[64,64,1024]{2,1,0:T(8,128)} %get-tuple-element.416, f32[1024,64]{0,1:T(8,128)S(1)} %dynamic-slice_bitcast_fusion.2), kind=kLoop, calls=%fused_computation.7.clone.1 | loop fusion | flops 8323072 | bytes 17301504 | tf_op jit(solution)/shard_map/while/body/eval_jaxpr/ijc,jc->ic/dot_general | solution.py:49
  380.1 8.4 %multiply_reduce_fusion.9 = f32[1024,64]{0,1:T(8,128)S(1)} fusion(f32[64,64,1024]{2,1,0:T(8,128)} %get-tuple-element.416, f32[1024,64]{0,1:T(8,128)S(1)} %dynamic-slice_bitcast_fusion.2), kind=kLoop, calls=%fused_computation.7.clone.1 | loop fusion | flops 8323072 | bytes 17301504 | tf_op jit(solution)/shard_map/while/body/eval_jaxpr/ijc,jc->ic/dot_general | solution.py:49
  391.3 8.4 %multiply_reduce_fusion.9 = f32[1024,64]{0,1:T(8,128)S(1)} fusion(f32[64,64,1024]{2,1,0:T(8,128)} %get-tuple-element.416, f32[1024,64]{0,1:T(8,128)S(1)} %dynamic-slice_bitcast_fusion.2), kind=kLoop, calls=%fused_computation.7.clone.1 | loop fusion | flops 8323072 | bytes 17301504 | tf_op jit(solution)/shard_map/while/body/eval_jaxpr/ijc,jc->ic/dot_general | solution.py:49
  413.8 8.4 %multiply_reduce_fusion.9 = f32[1024,64]{0,1:T(8,128)S(1)} fusion(f32[64,64,1024]{2,1,0:T(8,128)} %get-tuple-element.416, f32[1024,64]{0,1:T(8,128)S(1)} %dynamic-slice_bitcast_fusion.2), kind=kLoop, calls=%fused_computation.7.clone.1 | loop fusion | flops 8323072 | bytes 17301504 | tf_op jit(solution)/shard_map/while/body/eval_jaxpr/ijc,jc->ic/dot_general | solution.py:49
  425.0 8.4 %multiply_reduce_fusion.9 = f32[1024,64]{0,1:T(8,128)S(1)} fusion(f32[64,64,1024]{2,1,0:T(8,128)} %get-tuple-element.416, f32[1024,64]{0,1:T(8,128)S(1)} %dynamic-slice_bitcast_fusion.2), kind=kLoop, calls=%fused_computation.7.clone.1 | loop fusion | flops 8323072 | bytes 17301504 | tf_op jit(solution)/shard_map/while/body/eval_jaxpr/ijc,jc->ic/dot_general | solution.py:49
  436.3 8.4 %multiply_reduce_fusion.9 = f32[1024,64]{0,1:T(8,128)S(1)} fusion(f32[64,64,1024]{2,1,0:T(8,128)} %get-tuple-element.416, f32[1024,64]{0,1:T(8,128)S(1)} %dynamic-slice_bitcast_fusion.2), kind=kLoop, calls=%fused_computation.7.clone.1 | loop fusion | flops 8323072 | bytes 17301504 | tf_op jit(solution)/shard_map/while/body/eval_jaxpr/ijc,jc->ic/dot_general | solution.py:49
  456.7 10.6 %all-gather = f32[64,1024]{1,0:T(8,128)S(1)} all-gather(f32[16,1024]{1,0:T(8,128)S(1)} %get-tuple-element.106), channel_id=2, replica_groups=mesh['ctx'=4,'mp'=8] {'ctx'}, dimensions={0}, use_global_device_ids=true | all-gather | bytes 327680 | tf_op jit(solution)/shard_map/all_gather | solution.py:171
  467.5 10.9 %multiply_reduce_fusion.3 = f32[1024,512]{0,1:T(8,128)S(1)} fusion(f32[1024,16]{0,1:T(8,128)S(1)} %bitcast.107, f32[512]{0:T(512)S(1)} %iota_convert_fusion, f32[16,1024]{1,0:T(8,128)S(1)} %get-tuple-element.437, f32[16,1024]{1,0:T(8,128)S(1)} %get-tuple-element.433), kind=kLoop, calls=%fused_computation.14 | loop fusion | flops 33030144 | bytes 2295808 | tf_op jit(solution)/shard_map/inc,nc->ic/dot_general | solution.py:181
  (126 shorter events, 63.0 us)
Async XLA Ops:
  7.2 58.5 %copy-start = (bf16[512,1024]{1,0:T(8,128)(2,1)S(1)}, bf16[512,1024]{1,0:T(8,128)(2,1)}, u32[]{:S(2)}) copy-start(bf16[512,1024]{1,0:T(8,128)(2,1)} %param.16) | copy-start | bytes 3145732
  7.2 58.5 %all-gather.4.cloned.1.call-start = ((), (), s32[]{:S(2)}) async-start(), calls=%async_computation.1 | async-start | bytes 5242880 | tf_op jit(solution)/shard_map/all_gather | solution.py:96
  9.6 110.7 %all-gather.6.cloned.1.call-start = ((), (), s32[]{:S(2)}) async-start(), calls=%async_computation.2 | async-start | bytes 5242880 | tf_op jit(solution)/shard_map/all_gather | solution.py:97
  10.4 347.8 %reduce-scatter.2.cloned.1.call-start = ((), (), s32[]{:S(2)}) async-start(), calls=%async_computation.3 | async-start | bytes 9437184 | tf_op jit(solution)/shard_map/reduce_scatter | solution.py:149
  150.9 0.8 copy-start.4
  150.9 0.9 copy-start.7
  151.8 194.8 %copy-start.8 = (f32[3,1024]{1,0:T(4,128)S(1)}, f32[3,1024]{1,0:T(4,128)}, u32[]{:S(2)}) copy-start(f32[3,1024]{1,0:T(4,128)} %param.22) | copy-start | bytes 36868
  346.6 11.5 %copy-start.5 = (bf16[512,1024]{1,0:T(8,128)(2,1)S(1)}, bf16[512,1024]{1,0:T(8,128)(2,1)}, u32[]{:S(2)}) copy-start(bf16[512,1024]{1,0:T(8,128)(2,1)} %param.15) | copy-start | bytes 3145732
  359.8 7.0 %copy-start.2 = (bf16[512,1024]{1,0:T(8,128)(2,1)}, bf16[512,1024]{1,0:T(8,128)(2,1)S(1)}, u32[]{:S(2)}) copy-start(bf16[512,1024]{1,0:T(8,128)(2,1)S(1)} %fusion.21) | copy-start | bytes 3145732
  359.8 4.7 collective-permute-start
  467.4 10.9 %copy-start.3 = (f32[8,64,1024]{2,1,0:T(8,128)S(1)}, f32[8,64,1024]{2,1,0:T(8,128)}, u32[]{:S(2)}) copy-start(f32[8,64,1024]{2,1,0:T(8,128)} %get-tuple-element.105) | copy-start | bytes 6291460
  467.4 10.9 %copy-start.6 = (bf16[512,1024]{1,0:T(8,128)(2,1)S(1)}, bf16[512,1024]{1,0:T(8,128)(2,1)}, u32[]{:S(2)}) copy-start(bf16[512,1024]{1,0:T(8,128)(2,1)} %param.21) | copy-start | bytes 3145732
  467.5 10.9 %copy-start.9 = (f32[1024]{0:T(1024)S(1)}, f32[1024]{0:T(1024)}, u32[]{:S(2)}) copy-start(f32[1024]{0:T(1024)} %param.25) | copy-start | bytes 12292
  478.3 1.9 copy-start.1
Sparse Core Ops, SparseCore 0:
  10.4 55.2 all-gather.3
  67.6 52.7 all-gather.5
  151.1 89.5 reduce-scatter.1
where the time goes:
time: 488 us; the launch traced here: 487 us
  other arithmetic  329 us (67%)
  waiting for transfers between devices  77.7 us (16%)
  matrix products  48 us (10%)
  between operations  14 us (3%)
  blocking collectives  10.6 us (2%)
    add x16, other arithmetic, add_pole(): total + residue[None, None, :] * jnp.exp(-rate[None, None, :] * safe_diff...  193 us
    dot_general x8, other arithmetic, modal_step(): local = jnp.einsum('ijc,jc->ic', toeplitz, piece, precision=highest)  67.4 us
    all_gather x1, waiting for transfers between devices, attend(): lax.all_gather(key_rows, 'ctx', axis=0, tiled=True)  54.6 us
    all_gather x1, waiting for transfers between devices, attend(): lax.all_gather(value_rows, 'ctx', axis=0, tiled=True)  21.1 us
    dot_general x1, matrix products, update(): jnp.einsum('qhd,khd->hqk', queries, keys_here, preferred_element_type=jnp...  17.4 us
    dot_general x1, matrix products, update(): jnp.einsum('hqk,khd->hqd', weights.astype(jnp.bfloat16), values_here, pre...  16.6 us
    reduce_sum x1, other arithmetic, update(): new_total = running_total * rescale + jnp.sum(weights, axis=-1)  16.1 us
    dot_general x1, matrix products, per_device(): jnp.einsum('hqd,hdc->cq', heads_out, columns, preferred_element_type=jnp....  14 us
  transfers between devices with their start and end apart: 4, of which 3 were waited for; matrix products, arithmetic and copies ran while one was open for 49% of the time, Pallas kernels for 0%

commit v1 on v0

v1 whole, which is shorter than its diff:
```python
import functools
import math

import jax
import jax.numpy as jnp
from jax import lax
from jax.experimental import pallas as pl
from jax.experimental.pallas import tpu as pltpu
from jax.sharding import PartitionSpec as P

HD = 128
LANES = 128
CHUNKS = 8
masked_floor = -1e30


def causal_attention_kernel(query_ref, key_ref, value_ref, out_ref):
    length = query_ref.shape[0]
    block = min(256, length)
    factor = HD ** (-0.5) * math.log2(math.e)
    row = lax.broadcasted_iota(jnp.int32, (block, block), 0)
    column = lax.broadcasted_iota(jnp.int32, (block, block), 1)
    contract_last = (((1,), (1,)), ((), ()))
    for start in range(0, length, block):
        queries = query_ref[start : start + block, :]
        diagonal = lax.dot_general(
            queries,
            key_ref[start : start + block, :],
            contract_last,
            preferred_element_type=jnp.float32,
        )
        diagonal = jnp.where(column <= row, diagonal, masked_floor)
        highest = jnp.max(diagonal, axis=1, keepdims=True)
        if start:
            earlier = lax.dot_general(
                queries, key_ref[:start, :], contract_last, preferred_element_type=jnp.float32
            )
            highest = jnp.maximum(highest, jnp.max(earlier, axis=1, keepdims=True))
        shift = highest * factor
        weights = jnp.exp2(diagonal * factor - shift)
        total = jnp.sum(weights, axis=1, keepdims=True)
        summed = jnp.dot(
            weights.astype(jnp.bfloat16),
            value_ref[start : start + block, :],
            preferred_element_type=jnp.float32,
        )
        if start:
            weights = jnp.exp2(earlier * factor - shift)
            total = total + jnp.sum(weights, axis=1, keepdims=True)
            summed = summed + jnp.dot(
                weights.astype(jnp.bfloat16),
                value_ref[:start, :],
                preferred_element_type=jnp.float32,
            )
        out_ref[start : start + block, :] = (summed / total).astype(jnp.bfloat16)


def causal_attention(queries, keys, values):
    length, width = queries.shape
    heads = width // HD
    spec = pl.BlockSpec((length, HD), lambda head: (0, head))
    return pl.pallas_call(
        causal_attention_kernel,
        grid=(heads,),
        in_specs=[spec] * 3,
        out_specs=spec,
        out_shape=jax.ShapeDtypeStruct((length, width), jnp.bfloat16),
        compiler_params=pltpu.CompilerParams(vmem_limit_bytes=48 * 1024 * 1024),
        cost_estimate=pl.CostEstimate(
            flops=2 * length * length * width,
            bytes_accessed=8 * length * width,
            transcendentals=heads * length * length // 2,
        ),
    )(queries, keys, values)


def from_behind(value, axis, steps):
    count = lax.axis_size(axis)
    leading, last = (max(0, -steps), min(count, count - steps))
    return lax.ppermute(value, axis, [(source, source + steps) for source in range(leading, last)])


def attend(groups, key_rows, value_rows):
    width = key_rows.shape[1]
    heads = width // HD
    scale = HD ** (-0.5)
    query_sets = [(rows_q.reshape(rows_q.shape[0], heads, HD), pos_q) for rows_q, pos_q in groups]

    def update(state, queries, query_pos, keys_here, values_here, key_pos):
        running_top, running_total, running_sum = state
        scores = (
            jnp.einsum("qhd,khd->hqk", queries, keys_here, preferred_element_type=jnp.float32)
            * scale
        )
        allowed = (key_pos[None, :] <= query_pos[:, None])[None]
        masked = jnp.where(allowed, scores, masked_floor)
        new_top = jnp.maximum(running_top, jnp.max(masked, axis=-1))
        weights = jnp.where(allowed, jnp.exp(masked - new_top[..., None]), 0.0)
        rescale = jnp.exp(running_top - new_top)
        new_total = running_total * rescale + jnp.sum(weights, axis=-1)
        new_sum = running_sum * rescale[..., None] + jnp.einsum(
            "hqk,khd->hqd",
            weights.astype(jnp.bfloat16),
            values_here,
            preferred_element_type=jnp.float32,
        )
        return (new_top, new_total, new_sum)

    initial = tuple(
        (
            (
                jnp.full((heads, pos_q.shape[0]), masked_floor, jnp.float32),
                jnp.zeros((heads, pos_q.shape[0]), jnp.float32),
                jnp.zeros((heads, pos_q.shape[0], HD), jnp.float32),
            )
            for rows_q, pos_q in groups
        )
    )
    pieces = (
        lax.all_gather(key_rows, "ctx", axis=0, tiled=True),
        lax.all_gather(value_rows, "ctx", axis=0, tiled=True),
    )
    count = pieces[0].shape[0]
    blocks = count // count
    keys_all = pieces[0].reshape(blocks, count, heads, HD)
    values_all = pieces[1].reshape(blocks, count, heads, HD)
    index_rows = jnp.arange(count)
    pos_all = index_rows.reshape(blocks, count)

    def fold_step(states, block):
        keys_here, values_here, key_pos = block
        return (
            tuple(
                (
                    update(
                        states[g],
                        query_sets[g][0],
                        query_sets[g][1],
                        keys_here,
                        values_here,
                        key_pos,
                    )
                    for g in range(len(query_sets))
                )
            ),
            None,
        )

    result, _ = lax.scan(fold_step, initial, (keys_all, values_all, pos_all))
    return [(final[2] / final[1][..., None]).astype(jnp.bfloat16) for final in result]

def recurrence_states(signal_ref, rates_ref, ends_ref, state_ref):
    rows = signal_ref.shape[0]
    poles = rates_ref.shape[0]
    step = rows // CHUNKS
    decays = [
        jnp.broadcast_to(jnp.exp(-rates_ref[n : n + 1, :]), (CHUNKS, LANES)) for n in range(poles)
    ]

    def advance(i, states):
        piece = signal_ref[pl.ds(i, CHUNKS, stride=step), :]
        return tuple(decay * state + piece for decay, state in zip(decays, states))

    start = tuple(jnp.zeros((CHUNKS, LANES), jnp.float32) for _ in range(poles))
    ends = lax.fori_loop(0, step, advance, start, unroll=4)
    for n in range(poles):
        ends_ref[:, n, :] = ends[n]
    span = jnp.exp(-rates_ref[...] * float(step))
    total = jnp.zeros((poles, LANES), jnp.float32)
    for chunk in range(CHUNKS):
        total = span * total + ends_ref[chunk]
    state_ref[...] = total


def recurrence_outputs(signal_ref, rates_ref, residues_ref, ends_ref, before, conv_ref):
    rows = signal_ref.shape[0]
    poles = rates_ref.shape[0]
    step = rows // CHUNKS
    span = jnp.exp(-rates_ref[...] * float(step))
    for chunk in range(CHUNKS):
        here = ends_ref[chunk]
        ends_ref[chunk] = before
        before = span * before + here
    decays = [
        jnp.broadcast_to(jnp.exp(-rates_ref[n : n + 1, :]), (CHUNKS, LANES)) for n in range(poles)
    ]
    weights = [jnp.broadcast_to(residues_ref[n : n + 1, :], (CHUNKS, LANES)) for n in range(poles)]

    def advance(i, states):
        rows_here = pl.ds(i, CHUNKS, stride=step)
        piece = signal_ref[rows_here, :]
        states = tuple(decay * state + piece for decay, state in zip(decays, states))
        terms = [weight * state for weight, state in zip(weights, states)]
        while len(terms) > 1:
            terms = [sum(terms[i : i + 2][1:], terms[i]) for i in range(0, len(terms), 2)]
        conv_ref[rows_here, :] = terms[0]
        return states

    lax.fori_loop(0, step, advance, tuple(ends_ref[:, n, :] for n in range(poles)), unroll=2)


def make_signal(attended_ref, rim_ref, gate_ref, taps_ref, stream_ref, signal_ref):
    rows = attended_ref.shape[0]
    taps = taps_ref.shape[0]
    pad = rim_ref.shape[0]
    stream_ref[:pad, :] = rim_ref[...].astype(jnp.float32)
    stream_ref[pad:, :] = attended_ref[...].astype(jnp.float32)
    mixed = taps_ref[0:1, :] * stream_ref[pad : pad + rows, :]
    for tap in range(1, taps):
        mixed = mixed + taps_ref[tap : tap + 1, :] * stream_ref[pad - tap : pad - tap + rows, :]
    signal_ref[...] = gate_ref[...].astype(jnp.float32) * mixed


def states_kernel(attended_ref, rim_ref, gate_ref, taps_ref, rates_ref, signal_ref, ends_ref, state_ref, stream_ref):
    make_signal(attended_ref, rim_ref, gate_ref, taps_ref, stream_ref, signal_ref)
    recurrence_states(signal_ref, rates_ref, ends_ref, state_ref)


def outputs_kernel(signal_ref, ends_ref, before_ref, rates_ref, residues_ref, skip_ref, gate_ref, out_ref, held_ref, conv_ref):
    held_ref[...] = ends_ref[...]
    recurrence_outputs(signal_ref, rates_ref, residues_ref, held_ref, before_ref[...], conv_ref)
    mixed = conv_ref[...] + skip_ref[...] * signal_ref[...]
    out_ref[...] = (gate_ref[...].astype(jnp.float32) * mixed).astype(jnp.bfloat16)


def by_lanes(rows):
    return pl.BlockSpec((rows, LANES), lambda g: (0, g))


def hyena(attended, gate_in, gate_out, short_taps, decay_rates, residues, skip_gain):
    rows, width = attended.shape
    taps = short_taps.shape[0]
    poles = decay_rates.shape[0]
    segment = lax.axis_index("ctx")
    groups = width // LANES
    pad = 16
    rim = from_behind(attended[rows - pad :], "ctx", 1)
    ends_spec = pl.BlockSpec((CHUNKS, poles, LANES), lambda g: (0, 0, g))
    signal, ends, state = pl.pallas_call(
        states_kernel,
        grid=(groups,),
        in_specs=[by_lanes(rows), by_lanes(pad), by_lanes(rows), by_lanes(taps), by_lanes(poles)],
        out_specs=[by_lanes(rows), ends_spec, by_lanes(poles)],
        out_shape=[
            jax.ShapeDtypeStruct((rows, width), jnp.float32),
            jax.ShapeDtypeStruct((CHUNKS, poles, width), jnp.float32),
            jax.ShapeDtypeStruct((poles, width), jnp.float32),
        ],
        scratch_shapes=[pltpu.VMEM((pad + rows, LANES), jnp.float32)],
    )(attended, rim, gate_in, short_taps, decay_rates)
    states = lax.all_gather(state, "ctx", axis=0)
    earlier = jnp.arange(states.shape[0])
    gap = jnp.maximum((segment - earlier - 1) * rows, 0).astype(jnp.float32)
    factor = jnp.where(
        (earlier < segment)[:, None, None], jnp.exp(-decay_rates[None] * gap[:, None, None]), 0.0
    )
    before = jnp.sum(factor * states, axis=0)
    return pl.pallas_call(
        outputs_kernel,
        grid=(groups,),
        in_specs=[
            by_lanes(rows), ends_spec, by_lanes(poles), by_lanes(poles), by_lanes(poles), by_lanes(1), by_lanes(rows),
        ],
        out_specs=by_lanes(rows),
        out_shape=jax.ShapeDtypeStruct((rows, width), jnp.bfloat16),
        scratch_shapes=[
            pltpu.VMEM((CHUNKS, poles, LANES), jnp.float32),
            pltpu.VMEM((rows, LANES), jnp.float32),
        ],
    )(signal, ends, before, decay_rates, residues, skip_gain[None], gate_out)


def per_device(
    residual_in,
    query_rows,
    key_rows,
    value_rows,
    out_weight,
    gate_in,
    gate_out,
    short_taps,
    decay_rates,
    residues,
    skip_gain,
):
    rows, width = residual_in.shape
    segments = lax.axis_size("ctx")
    heads = width // HD
    if heads % segments == 0:
        spread = functools.partial(
            lax.all_to_all, axis_name="ctx", split_axis=1, concat_axis=0, tiled=True
        )
        own_heads = causal_attention(spread(query_rows), spread(key_rows), spread(value_rows))
        heads_out = lax.all_to_all(own_heads, "ctx", split_axis=0, concat_axis=1, tiled=True)
    else:
        query_pos = lax.axis_index("ctx") * rows + jnp.arange(rows)
        heads_out = attend([(query_rows, query_pos)], key_rows, value_rows)[0]
        heads_out = heads_out.transpose(1, 0, 2).reshape(rows, width)
    projected = lax.psum_scatter(
        jnp.einsum("qk,kc->cq", heads_out, out_weight, preferred_element_type=jnp.float32).astype(
            jnp.bfloat16
        ),
        "mp",
        scatter_dimension=0,
        tiled=True,
    ).astype(jnp.float32)
    attended = (residual_in.astype(jnp.float32) + projected.T).astype(jnp.bfloat16)
    hyena_out = hyena(attended, gate_in, gate_out, short_taps, decay_rates, residues, skip_gain)
    return (attended, hyena_out)


def solution(mesh):
    in_specs = (
        P("ctx", "mp"),
        P("ctx", "mp"),
        P("ctx", "mp"),
        P("ctx", "mp"),
        P("mp", None),
        P("ctx", "mp"),
        P("ctx", "mp"),
        P(None, "mp"),
        P(None, "mp"),
        P(None, "mp"),
        P("mp"),
    )
    out_specs = (P("ctx", "mp"), P("ctx", "mp"))
    return jax.shard_map(
        per_device, mesh=mesh, in_specs=in_specs, out_specs=out_specs, check_vma=False
    )
```

time: 488 us -> 239 us (0.49)
  other arithmetic: 329 us -> 2.37 us
  waiting for transfers between devices: 77.7 us -> 114 us
  matrix products: 48 us -> 17 us
  blocking collectives: 10.6 us -> 41.3 us
  Pallas kernels: 0 us -> 29.8 us
  starting transfers between devices: 3.45 us -> 12.1 us
    add x17 -> x0, other arithmetic: 193 us -> none  [the longest x16 193 us: add_pole(): total + residue[None, None, :] * jnp.exp(-rate[None, None, :] * safe_diff...]
    dot_general x25 -> x0, other arithmetic: 94.1 us -> none  [the longest x8 67.4 us: modal_step(): local = jnp.einsum('ijc,jc->ic', toeplitz, piece, precision=highest)]
    reduce_scatter x1, waiting for transfers between devices: 0.01 us -> 89.5 us  [per_device(): lax.psum_scatter(jnp.einsum('qk,kc->cq', heads_out, out_weight, preferred...]
    all_gather x2 -> x0, waiting for transfers between devices: 75.7 us -> none  [the longest x1 54.6 us: attend(): lax.all_gather(key_rows, 'ctx', axis=0, tiled=True)]
    dot_general x3 -> x1, matrix products: 48 us -> 17 us  [per_device(): jnp.einsum('qk,kc->cq', heads_out, out_weight, preferred_element_type=jnp...]
    all_to_all x0 -> x2, blocking collectives: none -> 30.6 us  [the longest x1 16 us: per_device(): spread(value_rows)]
    pallas_call x0 -> x3, Pallas kernels: none -> 29.8 us  [the longest x1 11.5 us: hyena(): pl.pallas_call(outputs_kernel, grid=(groups,), in_specs=[by_lanes(rows),...]
    all_to_all x0 -> x2, waiting for transfers between devices: none -> 23.1 us  [the longest x1 11.7 us: per_device(): spread(key_rows)]
  transfers between devices with their start and end apart: 4 -> 4, of which waited for: 3 -> 4; matrix products, arithmetic and copies ran while one was open for 49% -> 2% of each run, Pallas kernels for 0% -> 0%
where the time goes in v1:
time: 239 us; the launch traced here: 238 us
  waiting for transfers between devices  114 us (48%)
  blocking collectives  41.3 us (17%)
  Pallas kernels  29.8 us (12%)
  matrix products  17 us (7%)
  between operations  14.1 us (6%)
  starting transfers between devices  12.1 us (5%)
  local copies, waits for them, and re-layouts  6.98 us (3%)
    reduce_scatter x1, waiting for transfers between devices, per_device(): lax.psum_scatter(jnp.einsum('qk,kc->cq', heads_out, out_weight, preferred...  89.5 us
    dot_general x1, matrix products, per_device(): jnp.einsum('qk,kc->cq', heads_out, out_weight, preferred_element_type=jnp...  17 us
    all_to_all x1, blocking collectives, per_device(): spread(value_rows)  16 us
    all_to_all x1, blocking collectives, per_device(): lax.all_to_all(own_heads, 'ctx', split_axis=0, concat_axis=1, tiled=True)  14.6 us
    all_to_all x1, waiting for transfers between devices, per_device(): spread(key_rows)  11.7 us
    pallas_call x1, Pallas kernels, hyena(): pl.pallas_call(outputs_kernel, grid=(groups,), in_specs=[by_lanes(rows),...  11.5 us
    all_to_all x1, waiting for transfers between devices, per_device(): spread(query_rows)  11.4 us
    all_gather x1, blocking collectives, hyena(): states = lax.all_gather(state, 'ctx', axis=0)  10.7 us
  transfers between devices with their start and end apart: 4, of which 4 were waited for; matrix products, arithmetic and copies ran while one was open for 2% of the time, Pallas kernels for 0%

profile of v1, /device:TPU:0, one launch (start us, length us, event | category | flops | bytes accessed | tf_op | source)
XLA Modules:
  0.0 237.8 jit_solution(18058863860052446233)
XLA Ops:
  7.2 2.3 copy.28
  9.4 5.2 %all-to-all-start = ((bf16[512,4,256]{2,0,1:T(8,128)(2,1)}), bf16[512,4,256]{2,0,1:T(8,128)(2,1)S(1)}, u32[]{:S(2)}, u32[]{:S(2)}) async-start(bf16[512,4,256]{2,0,1:T(8,128)(2,1)} %bitcast.34), calls=%async_computation | async-start | bytes 2097152 | tf_op jit(solution)/shard_map/all_to_all | solution.py:293
  14.6 2.3 copy.27
  16.9 11.4 %all-to-all-done = bf16[512,4,256]{2,0,1:T(8,128)(2,1)S(1)} async-done(((bf16[512,4,256]{2,0,1:T(8,128)(2,1)}), bf16[512,4,256]{2,0,1:T(8,128)(2,1)S(1)}, u32[]{:S(2)}, u32[]{:S(2)}) %all-to-all-start) | async-done | bytes 1048608 | tf_op jit(solution)/shard_map/all_to_all | solution.py:293
  28.2 3.5 %all-to-all-start.1 = ((bf16[512,4,256]{2,0,1:T(8,128)(2,1)}), bf16[512,4,256]{2,0,1:T(8,128)(2,1)S(1)}, u32[]{:S(2)}, u32[]{:S(2)}) async-start(bf16[512,4,256]{2,0,1:T(8,128)(2,1)} %bitcast.33), calls=%async_computation.1 | async-start | bytes 2097152 | tf_op jit(solution)/shard_map/all_to_all | solution.py:293
  31.8 0.0 reduce-scatter.2.cloned.1.call-start
  31.8 1.3 copy.26
  33.1 11.7 %all-to-all-done.1 = bf16[512,4,256]{2,0,1:T(8,128)(2,1)S(1)} async-done(((bf16[512,4,256]{2,0,1:T(8,128)(2,1)}), bf16[512,4,256]{2,0,1:T(8,128)(2,1)S(1)}, u32[]{:S(2)}, u32[]{:S(2)}) %all-to-all-start.1) | async-done | bytes 1048608 | tf_op jit(solution)/shard_map/all_to_all | solution.py:293
  44.8 16.0 %all_to_all.76 = bf16[512,4,256]{2,0,1:T(8,128)(2,1)S(1)} all-to-all(bf16[512,4,256]{2,0,1:T(8,128)(2,1)S(1)} %bitcast.39), channel_id=1, replica_groups=mesh['ctx'=4,'mp'=8] {'ctx'}, dimensions={1} | all-to-all | bytes 2097152 | tf_op jit(solution)/shard_map/all_to_all | solution.py:293
  60.8 9.9 %shard_map.122 = bf16[2048,256]{1,0:T(8,128)(2,1)S(1)} custom-call(bf16[2048,256]{1,0:T(8,128)(2,1)S(1)} %bitcast.35, bf16[2048,256]{1,0:T(8,128)(2,1)S(1)} %bitcast.36, bf16[2048,256]{1,0:T(8,128)(2,1)S(1)} %bitcast.37), custom_call_target="tpu_custom_call" | custom-call | flops 2147483648 | bytes 4194304 | tf_op jit(solution)/shard_map/pallas_call | solution.py:62
  70.8 0.5 copy.19
  71.3 14.6 %all_to_all.77 = bf16[4,512,256]{1,2,0:T(8,128)(2,1)S(1)} all-to-all(bf16[4,512,256]{1,2,0:T(8,128)(2,1)S(1)} %copy.19), channel_id=1, replica_groups=mesh['ctx'=4,'mp'=8] {'ctx'}, dimensions={0} | all-to-all | bytes 2097152 | tf_op jit(solution)/shard_map/all_to_all | solution.py:294
  85.9 17.0 %fusion = bf16[8192,512]{0,1:T(8,128)(2,1)} fusion(bf16[512,1024]{0,1:T(8,128)(2,1)S(1)} %bitcast.44, bf16[1024,8192]{1,0:T(8,128)(2,1)} %param.15), kind=kOutput, calls=%fused_computation.1 | convolution fusion | flops 8594128896 | bytes 26214400 | tf_op jit(solution)/shard_map/qk,kc->cq/dot_general | solution.py:300
  102.9 0.0 copy-start.1
  102.9 0.0 copy-start.2
  102.9 0.0 reduce-scatter.2.cloned.1.call-update
  102.9 89.5 %reduce-scatter.2.cloned.1.call-done = bf16[1024,512]{0,1:T(8,128)(2,1)} async-done(((bf16[8192,512]{0,1:T(8,128)(2,1)}), bf16[1024,512]{0,1:T(8,128)(2,1)}) %reduce-scatter.2.cloned.1.call-update) | async-done | bytes 1048592 | tf_op jit(solution)/shard_map/reduce_scatter | solution.py:299
  192.4 0.0 copy-done.1
  192.4 1.6 fusion.1.attended_ref
  194.1 0.0 copy-start
  194.1 3.4 %collective-permute-start = (bf16[16,1024]{1,0:T(8,128)(2,1)S(1)}, bf16[16,1024]{1,0:T(8,128)(2,1)S(1)}, u32[]{:S(2)}, u32[]{:S(2)}) collective-permute-start(bf16[16,1024]{1,0:T(8,128)(2,1)S(1)} %slice.4), channel_id=1, source_target_pairs={{0,8},{8,16},{16,24},{1,9},{9,17},{17,25},{2,10},{10,18},{18,26},{... | collective-permute-start | bytes 98312 | tf_op jit(solution)/shard_map/ppermute | solution.py:80
  197.5 0.0 copy-done.2
  197.5 1.5 collective-permute-done.rim_ref
  199.1 0.0 copy-done
  199.1 0.0 copy-start.3
  199.1 0.6 copy-done.3
  199.7 8.3 %shard_map.123 = (f32[512,1024]{1,0:T(8,128)}, f32[8,16,1024]{2,1,0:T(8,128)}, f32[16,1024]{1,0:T(8,128)}) custom-call(bf16[512,1024]{1,0:T(8,128)(2,1)} %copy-done, bf16[16,1024]{1,0:T(8,128)(2,1)} %copy-done.3, bf16[512,1024]{1,0:T(8,128)(2,1)} %gate_ref.2, f32[3,1024]{1,0:T(4,128)} %taps_ref.1, f32[16,1024]{1,0:T(8,128)} %rates_ref.3), custom_call_target="tpu_custom_call" | custom-call | tf_op jit(solution)/shard_map/pallas_call | solution.py:239
  208.0 10.7 %all-gather = f32[64,1024]{1,0:T(8,128)S(1)} all-gather(f32[16,1024]{1,0:T(8,128)} %get-tuple-element.7), channel_id=2, replica_groups=mesh['ctx'=4,'mp'=8] {'ctx'}, dimensions={0}, use_global_device_ids=true | all-gather | bytes 327680 | tf_op jit(solution)/shard_map/all_gather | solution.py:251
  218.7 0.7 multiply_reduce_fusion.before_ref
  219.4 11.5 %shard_map.124 = bf16[512,1024]{1,0:T(8,128)(2,1)} custom-call(f32[512,1024]{1,0:T(8,128)} %get-tuple-element.5.signal_ref, f32[8,16,1024]{2,1,0:T(8,128)} %get-tuple-element.6.ends_ref, f32[16,1024]{1,0:T(8,128)} %multiply_reduce_fusion.before_ref, f32[16,1024]{1,0:T(8,128)} %rates_ref.3, f32[16,1024]{1,0:T(8,128)} %residues_ref.1, f32[1,1024]{1,0:T(1,128)} %bitcast.45, ...), custom_call_target="tpu_custom_call" | custom-call | tf_op jit(solution)/shard_map/pallas_call | solution.py:258
  (4 shorter events, 0.0 us)
Async XLA Ops:
  9.4 18.8 %all-to-all-start = ((bf16[512,4,256]{2,0,1:T(8,128)(2,1)}), bf16[512,4,256]{2,0,1:T(8,128)(2,1)S(1)}, u32[]{:S(2)}, u32[]{:S(2)}) async-start(bf16[512,4,256]{2,0,1:T(8,128)(2,1)} %bitcast.34), calls=%async_computation | async-start | bytes 2097152 | tf_op jit(solution)/shard_map/all_to_all | solution.py:293
  28.2 16.6 %all-to-all-start.1 = ((bf16[512,4,256]{2,0,1:T(8,128)(2,1)}), bf16[512,4,256]{2,0,1:T(8,128)(2,1)S(1)}, u32[]{:S(2)}, u32[]{:S(2)}) async-start(bf16[512,4,256]{2,0,1:T(8,128)(2,1)} %bitcast.33), calls=%async_computation.1 | async-start | bytes 2097152 | tf_op jit(solution)/shard_map/all_to_all | solution.py:293
  31.8 160.7 %reduce-scatter.2.cloned.1.call-start = ((), (), s32[]{:S(2)}) async-start(), calls=%async_computation.5 | async-start | bytes 9437184 | tf_op jit(solution)/shard_map/reduce_scatter | solution.py:299
  102.9 89.6 %copy-start.1 = (bf16[512,1024]{1,0:T(8,128)(2,1)S(1)}, bf16[512,1024]{1,0:T(8,128)(2,1)}, u32[]{:S(2)}) copy-start(bf16[512,1024]{1,0:T(8,128)(2,1)} %param.11) | copy-start | bytes 3145732
  102.9 94.6 %copy-start.2 = (f32[16,1024]{1,0:T(8,128)S(1)}, f32[16,1024]{1,0:T(8,128)}, u32[]{:S(2)}) copy-start(f32[16,1024]{1,0:T(8,128)} %rates_ref.3) | copy-start | bytes 196612
  194.1 5.0 %copy-start = (bf16[512,1024]{1,0:T(8,128)(2,1)}, bf16[512,1024]{1,0:T(8,128)(2,1)S(1)}, u32[]{:S(2)}) copy-start(bf16[512,1024]{1,0:T(8,128)(2,1)S(1)} %fusion.1.attended_ref) | copy-start | bytes 3145732
  194.1 5.0 %collective-permute-start = (bf16[16,1024]{1,0:T(8,128)(2,1)S(1)}, bf16[16,1024]{1,0:T(8,128)(2,1)S(1)}, u32[]{:S(2)}, u32[]{:S(2)}) collective-permute-start(bf16[16,1024]{1,0:T(8,128)(2,1)S(1)} %slice.4), channel_id=1, source_target_pairs={{0,8},{8,16},{16,24},{1,9},{9,17},{17,25},{2,10},{10,18},{18,26},{... | collective-permute-start | bytes 98312 | tf_op jit(solution)/shard_map/ppermute | solution.py:80
  199.1 0.6 copy-start.3
Sparse Core Ops, SparseCore 0:
  103.0 89.3 reduce-scatter.1

commit v2 on v1

--- a/solution.py
+++ b/solution.py
@@ -13,65 +13,346 @@
 CHUNKS = 8
 masked_floor = -1e30
 
-
-def causal_attention_kernel(query_ref, key_ref, value_ref, out_ref):
-    length = query_ref.shape[0]
-    block = min(256, length)
+MESH = pl.DeviceIdType.MESH
+
+
+def attend_block(query_ref, key_ref, value_ref, out_ref, start, block):
     factor = HD ** (-0.5) * math.log2(math.e)
     row = lax.broadcasted_iota(jnp.int32, (block, block), 0)
     column = lax.broadcasted_iota(jnp.int32, (block, block), 1)
     contract_last = (((1,), (1,)), ((), ()))
-    for start in range(0, length, block):
-        queries = query_ref[start : start + block, :]
-        diagonal = lax.dot_general(
-            queries,
-            key_ref[start : start + block, :],
-            contract_last,
-            preferred_element_type=jnp.float32,
-        )
-        diagonal = jnp.where(column <= row, diagonal, masked_floor)
-        highest = jnp.max(diagonal, axis=1, keepdims=True)
-        if start:
-            earlier = lax.dot_general(
-                queries, key_ref[:start, :], contract_last, preferred_element_type=jnp.float32
+    queries = query_ref[start : start + block, :]
+    diagonal = lax.dot_general(
+        queries,
+        key_ref[start : start + block, :],
+        contract_last,
+        preferred_element_type=jnp.float32,
+    )
+    diagonal = jnp.where(column <= row, diagonal, masked_floor)
+    highest = jnp.max(diagonal, axis=1, keepdims=True)
+    if start:
+        earlier = lax.dot_general(
+            queries, key_ref[:start, :], contract_last, preferred_element_type=jnp.float32
+        )
+        highest = jnp.maximum(highest, jnp.max(earlier, axis=1, keepdims=True))
+    shift = highest * factor
+    weights = jnp.exp2(diagonal * factor - shift)
+    total = jnp.sum(weights, axis=1, keepdims=True)
+    summed = jnp.dot(
+        weights.astype(jnp.bfloat16),
+        value_ref[start : start + block, :],
+        preferred_element_type=jnp.float32,
+    )
+    if start:
+        weights = jnp.exp2(earlier * factor - shift)
+        total = total + jnp.sum(weights, axis=1, keepdims=True)
+        summed = summed + jnp.dot(
+            weights.astype(jnp.bfloat16), value_ref[:start, :], preferred_element_type=jnp.float32
+        )
+    out_ref[start : start + block, :] = (summed / total).astype(jnp.bfloat16)
+
+
+def spread_attention_kernel(
+    n, block, query_ref, key_ref, value_ref, out_ref,
+    queries, keys, values, results, send, recv, own, back_send, back_recv, back_own,
+):
+    me = lax.axis_index("ctx")
+    rows = query_ref.shape[0]
+    heads = queries.shape[0]
+    barrier = pltpu.get_barrier_semaphore()
+    for p in range(1, n):
+        pl.semaphore_signal(
+            barrier, inc=1, device_id={"ctx": lax.rem(me + p, n)}, device_id_type=MESH
+        )
+    pl.semaphore_wait(barrier, n - 1)
+
+    sources = (key_ref, query_ref, value_ref)
+    slots = (keys, queries, values)
+    my_rows = pl.ds(pl.multiple_of(me * rows, rows), rows)
+    arrivals = []
+    own_copies = []
+    for head in range(heads):
+        arrivals.append([])
+        own_copies.append([])
+        for t in range(3):
+            for p in range(n):
+                target = lax.rem(me + p, n)
+                columns = pl.ds(pl.multiple_of((target * heads + head) * HD, HD), HD)
+                source = sources[t].at[:, columns]
+                landing = slots[t].at[head, my_rows, :]
+                if p == 0:
+                    copy = pltpu.make_async_copy(source, landing, own.at[head, t])
+                    own_copies[head].append(copy)
+                else:
+                    copy = pltpu.make_async_remote_copy(
+                        src_ref=source,
+                        dst_ref=landing,
+                        send_sem=send.at[head, t, p],
+                        recv_sem=recv.at[head, t, p],
+                        device_id={"ctx": target},
+                        device_id_type=MESH,
+                    )
+                    arrivals[head].append(copy)
+                copy.start()
+
+    returned = []
+    for head in range(heads):
+        for copy in own_copies[head]:
+            copy.wait()
+        for copy in arrivals[head]:
+            copy.wait_recv()
+        columns = pl.ds(pl.multiple_of((me * heads + head) * HD, HD), HD)
+        landing = out_ref.at[:, columns]
+        for segment in range(n):
+            for start in range(segment * rows, (segment + 1) * rows, block):
+                attend_block(
+                    queries.at[head], keys.at[head], values.at[head], results.at[head], start, block
+                )
+            source = results.at[head, pl.ds(segment * rows, rows), :]
+            away = lax.rem(segment - me + n, n)
+
+            @pl.when(away != 0)
+            def _():
+                pltpu.make_async_remote_copy(
+                    src_ref=source,
+                    dst_ref=landing,
+                    send_sem=back_send.at[head, away],
+                    recv_sem=back_recv.at[head, away],
+                    device_id={"ctx": segment},
+                    device_id_type=MESH,
+                ).start()
+
+            @pl.when(away == 0)
+            def _():
+                pltpu.make_async_copy(source, landing, back_own.at[head]).start()
+
+    for head in range(heads):
+        source = results.at[head, pl.ds(0, rows), :]
+        landing = out_ref.at[:, pl.ds(0, HD)]
+        pltpu.make_async_copy(source, landing, back_own.at[head]).wait()
+        for p in range(1, n):
+            copy = pltpu.make_async_remote_copy(
+                src_ref=source,
+                dst_ref=landing,
+                send_sem=back_send.at[head, p],
+                recv_sem=back_recv.at[head, p],
+                device_id={"ctx": lax.rem(me + p, n)},
+                device_id_type=MESH,
             )
-            highest = jnp.maximum(highest, jnp.max(earlier, axis=1, keepdims=True))
-        shift = highest * factor
-        weights = jnp.exp2(diagonal * factor - shift)
-        total = jnp.sum(weights, axis=1, keepdims=True)
-        summed = jnp.dot(
-            weights.astype(jnp.bfloat16),
-            value_ref[start : start + block, :],
-            preferred_element_type=jnp.float32,
-        )
-        if start:
-            weights = jnp.exp2(earlier * factor - shift)
-            total = total + jnp.sum(weights, axis=1, keepdims=True)
-            summed = summed + jnp.dot(
-                weights.astype(jnp.bfloat16),
-                value_ref[:start, :],
-                preferred_element_type=jnp.float32,
-            )
-        out_ref[start : start + block, :] = (summed / total).astype(jnp.bfloat16)
-
-
-def causal_attention(queries, keys, values):
-    length, width = queries.shape
-    heads = width // HD
-    spec = pl.BlockSpec((length, HD), lambda head: (0, head))
+            copy.wait_send()
+            copy.wait_recv()
+        for copy in arrivals[head]:
+            copy.wait_send()
+
+
+def spread_attention(query_rows, key_rows, value_rows):
+    rows, width = query_rows.shape
+    n = lax.axis_size("ctx")
+    heads = width // HD // n
+    length = n * rows
+    whole = pltpu.VMEM((heads, length, HD), jnp.bfloat16)
+    dma = pltpu.SemaphoreType.DMA
     return pl.pallas_call(
-        causal_attention_kernel,
-        grid=(heads,),
-        in_specs=[spec] * 3,
-        out_specs=spec,
-        out_shape=jax.ShapeDtypeStruct((length, width), jnp.bfloat16),
-        compiler_params=pltpu.CompilerParams(vmem_limit_bytes=48 * 1024 * 1024),
+        functools.partial(spread_attention_kernel, n, min(256, rows)),
+        in_specs=[pl.BlockSpec(memory_space=pl.ANY)] * 3,
+        out_specs=pl.BlockSpec(memory_space=pl.ANY),
+        out_shape=jax.ShapeDtypeStruct((rows, width), jnp.bfloat16),
+        scratch_shapes=[
+            whole, whole, whole, whole,
+            dma((heads, 3, n)), dma((heads, 3, n)), dma((heads, 3)),
+            dma((heads, n)), dma((heads, n)), dma((heads,)),
+        ],
+        compiler_params=pltpu.CompilerParams(
+            collective_id=1, has_side_effects=True, vmem_limit_bytes=48 * 1024 * 1024
+        ),
         cost_estimate=pl.CostEstimate(
-            flops=2 * length * length * width,
-            bytes_accessed=8 * length * width,
+            flops=2 * length * length * heads * HD,
+            bytes_accessed=8 * rows * width,
             transcendentals=heads * length * length // 2,
         ),
-    )(queries, keys, values)
+    )(query_rows, key_rows, value_rows)
+
+
+def project_reduce_kernel(
+    heads_ref, residual_ref, weight_ref, out_ref,
+    weights, for_pair, from_pair, sums, from_end, from_mid,
+    weight_sem, pair_send, pair_recv, end_send, end_recv, mid_send, mid_recv, back_send,
+):
+    mp = lax.axis_index("mp")
+    core = lax.rem(mp, 2)
+    chip = mp // 2
+    mirrored = chip >= 2
+    middle = jnp.logical_or(chip == 1, chip == 2)
+    step = jnp.where(mirrored, -1, 1)
+    pair = chip * 2 + 1 - core
+    toward = (chip + step) * 2 + core
+    behind = (chip - step) * 2 + core
+    rows, width = residual_ref.shape
+    parts = end_send.shape[1]
+    part = rows // parts
+    tile = min(256, width)
+
+    copies = []
+    for k in range(4):
+        target = jnp.where(mirrored, k, 3 - k)
+        for mine in range(2):
+            owner = target * 2 + (core if mine else 1 - core)
+            columns = pl.ds(pl.multiple_of(owner * width, width), width)
+            copy = pltpu.make_async_copy(
+                weight_ref.at[:, columns], weights.at[k, mine], weight_sem.at[k, mine]
+            )
+            copy.start()
+            copies.append(copy)
+
+    barrier = pltpu.get_barrier_semaphore()
+    pl.semaphore_signal(barrier, inc=1, device_id={"mp": pair}, device_id_type=MESH)
+    pl.semaphore_signal(barrier, inc=1, device_id={"mp": toward}, device_id_type=MESH)
+
+    @pl.when(middle)
+    def _():
+        pl.semaphore_signal(barrier, inc=1, device_id={"mp": behind}, device_id_type=MESH)
+        pl.semaphore_wait(barrier, 3)
+
+    @pl.when(jnp.logical_not(middle))
+    def _():
+        pl.semaphore_wait(barrier, 2)
+
+    def part_copy(source, landing, slot, h, send_sem, recv_sem, device):
+        piece = pl.ds(h * part, part)
+        return pltpu.make_async_remote_copy(
+            src_ref=sums.at[source, piece, :],
+            dst_ref=landing.at[slot, piece, :],
+            send_sem=send_sem,
+            recv_sem=recv_sem,
+            device_id={"mp": device},
+            device_id_type=MESH,
+        )
+
+    def to_middle(k, h):
+        return part_copy(k, from_end, k, h, end_send.at[k, h], end_recv.at[k, h], toward)
+
+    def across(k, h):
+        return part_copy(k, from_mid, k, h, mid_send.at[k, h], mid_recv.at[k, h], toward)
+
+    def to_end(h):
+        return part_copy(3, from_mid, 0, h, back_send.at[h], mid_recv.at[0, h], behind)
+
+    pair_copies = []
+    for k in range(4):
+        copies[2 * k].wait()
+
+        @pl.loop(0, width // tile)
+        def _(j):
+            columns = pl.ds(pl.multiple_of(j * tile, tile), tile)
+            for_pair[k, :, columns] = jnp.dot(
+                heads_ref[...], weights[k, 0, :, columns], preferred_element_type=jnp.float32
+            ).astype(jnp.bfloat16)
+
+        copy = pltpu.make_async_remote_copy(
+            src_ref=for_pair.at[k],
+            dst_ref=from_pair.at[k],
+            send_sem=pair_send.at[k],
+            recv_sem=pair_recv.at[k],
+            device_id={"mp": pair},
+            device_id_type=MESH,
+        )
+        copy.start()
+        pair_copies.append(copy)
+        copies[2 * k + 1].wait()
+        copy.wait_recv()
+
+        @pl.loop(0, width // tile)
+        def _(j):
+            columns = pl.ds(pl.multiple_of(j * tile, tile), tile)
+            mixed = jnp.dot(
+                heads_ref[...], weights[k, 1, :, columns], preferred_element_type=jnp.float32
+            )
+            sums[k, :, columns] = (mixed + from_pair[k, :, columns].astype(jnp.float32)).astype(
+                jnp.bfloat16
+            )
+
+        if k < 3:
+
+            @pl.when(jnp.logical_not(middle))
+            def _():
+                for h in range(parts):
+                    to_middle(k, h).start()
+
+    def add(k, h, landing, slot):
+        piece = pl.ds(h * part, part)
+        total = sums[k, piece, :].astype(jnp.float32) + landing[slot, piece, :].astype(jnp.float32)
+        sums[k, piece, :] = total.astype(jnp.bfloat16)
+
+    def finish(h, k, landings):
+        piece = pl.ds(h * part, part)
+        total = sums[k, piece, :].astype(jnp.float32)
+        for landing, slot in landings:
+            total = total + landing[slot, piece, :].astype(jnp.float32)
+        out_ref[piece, :] = (residual_ref[piece, :].astype(jnp.float32) + total).astype(jnp.bfloat16)
+
+    @pl.when(middle)
+    def _():
+        for k in range(2):
+            for h in range(parts):
+                to_middle(k, h).wait_recv()
+                add(k, h, from_end, k)
+                across(k, h).start()
+        for h in range(parts):
+            across(0, h).wait_recv()
+            add(3, h, from_mid, 0)
+            to_end(h).start()
+        for h in range(parts):
+            to_middle(2, h).wait_recv()
+            across(1, h).wait_recv()
+            finish(h, 2, ((from_end, 2), (from_mid, 1)))
+        for h in range(parts):
+            across(0, h).wait_send()
+            across(1, h).wait_send()
+            to_end(h).wait_send()
+
+    @pl.when(jnp.logical_not(middle))
+    def _():
+        for h in range(parts):
+            across(0, h).wait_recv()
+            finish(h, 3, ((from_mid, 0),))
+        for k in range(3):
+            for h in range(parts):
+                to_middle(k, h).wait_send()
+
+    for copy in pair_copies:
+        copy.wait_send()
+
+
+def project_reduce(heads_out, residual_in, out_weight):
+    rows, width = residual_in.shape
+    depth = heads_out.shape[1]
+    parts = 4 if rows % 64 == 0 else 1
+    vmem = pl.BlockSpec(memory_space=pltpu.VMEM)
+    dma = pltpu.SemaphoreType.DMA
+
+    def blocks(count):
+        return pltpu.VMEM((count, rows, width), jnp.bfloat16)
+
+    return pl.pallas_call(
+        project_reduce_kernel,
+        in_specs=[vmem, vmem, pl.BlockSpec(memory_space=pl.ANY)],
+        out_specs=vmem,
+        out_shape=jax.ShapeDtypeStruct((rows, width), jnp.bfloat16),
+        scratch_shapes=[
+            pltpu.VMEM((4, 2, depth, width), jnp.bfloat16),
+            blocks(4), blocks(4), blocks(4), blocks(3), blocks(2),
+            dma((4, 2)), dma((4,)), dma((4,)),
+            dma((3, parts)), dma((3, parts)), dma((2, parts)), dma((2, parts)), dma((parts,)),
+        ],
+        compiler_params=pltpu.CompilerParams(
+            collective_id=2, has_side_effects=True, vmem_limit_bytes=56 * 1024 * 1024
+        ),
+        cost_estimate=pl.CostEstimate(
+            flops=16 * rows * depth * width,
+            bytes_accessed=16 * depth * width + 6 * rows * width,
+            transcendentals=0,
+        ),
+    )(heads_out, residual_in, out_weight)
 
 
 def from_behind(value, axis, steps):
@@ -287,24 +568,21 @@
     segments = lax.axis_size("ctx")
     heads = width // HD
     if heads % segments == 0:
-        spread = functools.partial(
-            lax.all_to_all, axis_name="ctx", split_axis=1, concat_axis=0, tiled=True
-        )
-        own_heads = causal_attention(spread(query_rows), spread(key_rows), spread(value_rows))
-        heads_out = lax.all_to_all(own_heads, "ctx", split_axis=0, concat_axis=1, tiled=True)
+        heads_out = spread_attention(query_rows, key_rows, value_rows)
     else:
         query_pos = lax.axis_index("ctx") * rows + jnp.arange(rows)
         heads_out = attend([(query_rows, query_pos)], key_rows, value_rows)[0]
         heads_out = heads_out.transpose(1, 0, 2).reshape(rows, width)
-    projected = lax.psum_scatter(
-        jnp.einsum("qk,kc->cq", heads_out, out_weight, preferred_element_type=jnp.float32).astype(
-            jnp.bfloat16
-        ),
-        "mp",
-        scatter_dimension=0,
-        tiled=True,
-    ).astype(jnp.float32)
-    attended = (residual_in.astype(jnp.float32) + projected.T).astype(jnp.bfloat16)
+    if lax.axis_size("mp") == 8:
+        attended = project_reduce(heads_out, residual_in, out_weight)
+    else:
+        partial = jnp.einsum(
+            "qk,kc->cq", heads_out, out_weight, preferred_element_type=jnp.float32
+        ).astype(jnp.bfloat16)
+        projected = lax.psum_scatter(partial, "mp", scatter_dimension=0, tiled=True)
+        attended = (
+            residual_in.astype(jnp.float32) + projected.astype(jnp.float32).T
+        ).astype(jnp.bfloat16)
     hyena_out = hyena(attended, gate_in, gate_out, short_taps, decay_rates, residues, skip_gain)
     return (attended, hyena_out)
 

time: 239 us -> 180 us (0.75)
  Pallas kernels: 29.8 us -> 153 us
  waiting for transfers between devices: 114 us -> 1.66 us
  blocking collectives: 41.3 us -> 13.6 us
  matrix products: 17 us -> 0 us
  between operations: 14.1 us -> 0.71 us
  starting transfers between devices: 12.1 us -> 1.59 us
    pallas_call x1 -> x2, Pallas kernels: 9.93 us -> 133 us  [the longest x1 82.3 us: project_reduce(): pl.pallas_call(project_reduce_kernel, in_specs=[vmem, vmem, pl.BlockSpec(...]
    reduce_scatter x1 -> x0, waiting for transfers between devices: 89.5 us -> none  [per_device(): lax.psum_scatter(jnp.einsum('qk,kc->cq', heads_out, out_weight, preferred...]
    all_to_all x2 -> x0, blocking collectives: 30.6 us -> none  [the longest x1 16 us: per_device(): spread(value_rows)]
    all_to_all x2 -> x0, waiting for transfers between devices: 23.1 us -> none  [the longest x1 11.7 us: per_device(): spread(key_rows)]
    dot_general x1 -> x0, matrix products: 17 us -> none  [per_device(): jnp.einsum('qk,kc->cq', heads_out, out_weight, preferred_element_type=jnp...]
    all_to_all x2 -> x0, starting transfers between devices: 8.68 us -> none  [the longest x1 5.16 us: per_device(): spread(query_rows)]
    unnamed x8 -> x13, local copies, waits for them, and re-layouts: 0.61 us -> 7.5 us
    all_to_all x4 -> x0, local copies, waits for them, and re-layouts: 6.36 us -> none  [the longest x1 2.26 us: per_device(): spread(query_rows)]
  transfers between devices with their start and end apart: 4 -> 1, of which waited for: 4 -> 1; matrix products, arithmetic and copies ran while one was open for 2% -> 0% of each run, Pallas kernels for 0% -> 0%
where the time goes in v2:
time: 180 us; the launch traced here: 179 us
  Pallas kernels  153 us (85%)
  blocking collectives  13.6 us (8%)
  local copies, waits for them, and re-layouts  8.26 us (5%)
    pallas_call x1, Pallas kernels, project_reduce(): pl.pallas_call(project_reduce_kernel, in_specs=[vmem, vmem, pl.BlockSpec(...  82.3 us
    pallas_call x1, Pallas kernels, spread_attention(): pl.pallas_call(functools.partial(spread_attention_kernel, n, min(256, row...  50.5 us
    all_gather x1, blocking collectives, hyena(): states = lax.all_gather(state, 'ctx', axis=0)  13.6 us
    pallas_call x1, Pallas kernels, hyena(): pl.pallas_call(outputs_kernel, grid=(groups,), in_specs=[by_lanes(rows),...  11.5 us
    pallas_call x1, Pallas kernels, hyena(): pl.pallas_call(states_kernel, grid=(groups,), in_specs=[by_lanes(rows), b...  8.31 us
    unnamed x13, local copies, waits for them, and re-layouts  7.5 us
  transfers between devices with their start and end apart: 1, of which 1 were waited for; matrix products, arithmetic and copies ran while one was open for 0% of the time, Pallas kernels for 0%

profile of v2, /device:TPU:0, one launch (start us, length us, event | category | flops | bytes accessed | tf_op | source)
XLA Modules:
  0.0 179.1 jit_solution(14331297651034687573)
XLA Ops:
  0.6 0.0 copy-start
  0.6 1.2 copy-done
  1.9 0.0 copy-start.1
  1.9 1.2 copy-done.1
  3.1 0.0 copy-start.2
  3.1 1.2 copy-done.2
  4.3 50.5 %shard_map.122.heads_ref = bf16[512,1024]{1,0:T(8,128)(2,1)S(1)} custom-call(bf16[512,1024]{1,0:T(8,128)(2,1)S(1)} %copy-done, bf16[512,1024]{1,0:T(8,128)(2,1)S(1)} %copy-done.1, bf16[512,1024]{1,0:T(8,128)(2,1)S(1)} %copy-done.2), custom_call_target="tpu_custom_call" | custom-call | flops 2147483648 | bytes 4194304 | tf_op jit(solution)/shard_map/pallas_call | solution.py:155
  54.8 0.0 copy-start.3
  54.8 1.0 copy-done.3
  55.8 0.0 copy-start.4
  55.8 82.3 %shard_map.123.attended_ref = bf16[512,1024]{1,0:T(8,128)(2,1)} custom-call(bf16[512,1024]{1,0:T(8,128)(2,1)} %copy-done.3, bf16[512,1024]{1,0:T(8,128)(2,1)} %residual_ref.1, bf16[1024,8192]{1,0:T(8,128)(2,1)} %weight_ref.1), custom_call_target="tpu_custom_call" | custom-call | flops 8589934592 | bytes 19922944 | tf_op jit(solution)/shard_map/pallas_call | solution.py:336
  138.0 0.8 slice.3
  138.8 1.6 collective-permute-start
  140.4 0.0 copy-done.4
  140.5 1.7 collective-permute-done.rim_ref
  142.1 0.0 copy-start.5
  142.1 0.6 copy-done.5
  142.7 8.3 %shard_map.124 = (f32[512,1024]{1,0:T(8,128)}, f32[8,16,1024]{2,1,0:T(8,128)}, f32[16,1024]{1,0:T(8,128)}) custom-call(bf16[512,1024]{1,0:T(8,128)(2,1)} %shard_map.123.attended_ref, bf16[16,1024]{1,0:T(8,128)(2,1)} %copy-done.5, bf16[512,1024]{1,0:T(8,128)(2,1)} %gate_ref.2, f32[3,1024]{1,0:T(4,128)} %taps_ref.1, f32[16,1024]{1,0:T(8,128)} %rates_ref.3), custom_call_target="tpu_custom_call" | custom-call | tf_op jit(solution)/shard_map/pallas_call | solution.py:520
  151.0 13.6 %all-gather = f32[64,1024]{1,0:T(8,128)S(1)} all-gather(f32[16,1024]{1,0:T(8,128)} %get-tuple-element.7), channel_id=2, replica_groups=mesh['ctx'=4,'mp'=8] {'ctx'}, dimensions={0}, use_global_device_ids=true | all-gather | bytes 327680 | tf_op jit(solution)/shard_map/all_gather | solution.py:532
  164.6 0.7 multiply_reduce_fusion.before_ref
  165.3 11.5 %shard_map.125 = bf16[512,1024]{1,0:T(8,128)(2,1)} custom-call(f32[512,1024]{1,0:T(8,128)} %get-tuple-element.5.signal_ref, f32[8,16,1024]{2,1,0:T(8,128)} %get-tuple-element.6.ends_ref, f32[16,1024]{1,0:T(8,128)} %multiply_reduce_fusion.before_ref, f32[16,1024]{1,0:T(8,128)} %rates_ref.3, f32[16,1024]{1,0:T(8,128)} %residues_ref.1, f32[1,1024]{1,0:T(1,128)} %bitcast.3, ...), custom_call_target="tpu_custom_call" | custom-call | tf_op jit(solution)/shard_map/pallas_call | solution.py:539
  176.9 2.3 %copy.14 = bf16[512,1024]{1,0:T(8,128)(2,1)} copy(bf16[512,1024]{1,0:T(8,128)(2,1)} %shard_map.123.attended_ref) | data formatting | bytes 2097152
  (3 shorter events, 0.0 us)
Async XLA Ops:
  0.6 1.2 copy-start
  1.9 1.2 copy-start.1
  3.1 1.2 copy-start.2
  54.8 1.0 copy-start.3
  55.8 84.7 %copy-start.4 = (f32[16,1024]{1,0:T(8,128)S(1)}, f32[16,1024]{1,0:T(8,128)}, u32[]{:S(2)}) copy-start(f32[16,1024]{1,0:T(8,128)} %rates_ref.3) | copy-start | bytes 196612
  138.8 3.3 %collective-permute-start = (bf16[16,1024]{1,0:T(8,128)(2,1)S(1)}, bf16[16,1024]{1,0:T(8,128)(2,1)S(1)}, u32[]{:S(2)}, u32[]{:S(2)}) collective-permute-start(bf16[16,1024]{1,0:T(8,128)(2,1)S(1)} %slice.3), channel_id=1, source_target_pairs={{0,8},{8,16},{16,24},{1,9},{9,17},{17,25},{2,10},{10,18},{18,26},{... | collective-permute-start | bytes 98312 | tf_op jit(solution)/shard_map/ppermute | solution.py:361
  142.1 0.6 copy-start.5

commit v3 on v2

--- a/solution.py
+++ b/solution.py
@@ -173,10 +173,13 @@
     )(query_rows, key_rows, value_rows)
 
 
-def project_reduce_kernel(
-    heads_ref, residual_ref, weight_ref, out_ref,
+def project_hyena_kernel(
+    n, heads_ref, residual_ref, weight_ref, gate_in_ref, gate_out_ref, taps_ref, rates_ref,
+    residues_ref, skip_ref, out_ref, hyena_ref,
     weights, for_pair, from_pair, sums, from_end, from_mid,
+    rim, stream, signal, conv, ends, state_out, states_in,
     weight_sem, pair_send, pair_recv, end_send, end_recv, mid_send, mid_recv, back_send,
+    rim_send, rim_recv, state_send, state_recv,
 ):
     mp = lax.axis_index("mp")
     core = lax.rem(mp, 2)
@@ -187,172 +190,284 @@
     pair = chip * 2 + 1 - core
     toward = (chip + step) * 2 + core
     behind = (chip - step) * 2 + core
+    segment = lax.axis_index("ctx")
     rows, width = residual_ref.shape
     parts = end_send.shape[1]
-    part = rows // parts
-    tile = min(256, width)
-
-    copies = []
-    for k in range(4):
-        target = jnp.where(mirrored, k, 3 - k)
+    part = width // parts
+    poles = rates_ref.shape[0]
+    pad = rim.shape[0]
+
+    for p in range(1, n):
+
+        @pl.when(segment < p)
+        def _():
+            states_in[p] = jnp.zeros(states_in.shape[1:], jnp.float32)
+
+    @pl.when(segment == 0)
+    def _():
+        rim[...] = jnp.zeros(rim.shape, rim.dtype)
+
+    copies = {}
+    for h in range(parts):
         for mine in range(2):
-            owner = target * 2 + (core if mine else 1 - core)
-            columns = pl.ds(pl.multiple_of(owner * width, width), width)
-            copy = pltpu.make_async_copy(
-                weight_ref.at[:, columns], weights.at[k, mine], weight_sem.at[k, mine]
-            )
-            copy.start()
-            copies.append(copy)
+            for k in range(4):
+                target = jnp.where(mirrored, k, 3 - k)
+                owner = target * 2 + (core if mine else 1 - core)
+                columns = pl.ds(pl.multiple_of(owner * width + h * part, part), part)
+                copies[h, k, mine] = pltpu.make_async_copy(
+                    weight_ref.at[:, columns],
+                    weights.at[k, mine, :, pl.ds(h * part, part)],
+                    weight_sem.at[h, k, mine],
+                )
+                copies[h, k, mine].start()
 
     barrier = pltpu.get_barrier_semaphore()
+    for p in range(1, n):
+        pl.semaphore_signal(
+            barrier, inc=1, device_id={"ctx": lax.rem(segment + p, n)}, device_id_type=MESH
+        )
     pl.semaphore_signal(barrier, inc=1, device_id={"mp": pair}, device_id_type=MESH)
     pl.semaphore_signal(barrier, inc=1, device_id={"mp": toward}, device_id_type=MESH)
 
     @pl.when(middle)
     def _():
         pl.semaphore_signal(barrier, inc=1, device_id={"mp": behind}, device_id_type=MESH)
-        pl.semaphore_wait(barrier, 3)
+        pl.semaphore_wait(barrier, 3 + n - 1)
 
     @pl.when(jnp.logical_not(middle))
     def _():
-        pl.semaphore_wait(barrier, 2)
+        pl.semaphore_wait(barrier, 2 + n - 1)
+
+    def cut(h):
+        return pl.ds(h * part, part)
 
     def part_copy(source, landing, slot, h, send_sem, recv_sem, device):
-        piece = pl.ds(h * part, part)
         return pltpu.make_async_remote_copy(
-            src_ref=sums.at[source, piece, :],
-            dst_ref=landing.at[slot, piece, :],
+            src_ref=source.at[slot[0], :, cut(h)],
+            dst_ref=landing.at[slot[1], :, cut(h)],
             send_sem=send_sem,
             recv_sem=recv_sem,
             device_id={"mp": device},
             device_id_type=MESH,
         )
 
+    def to_pair(k, h):
+        return part_copy(
+            for_pair, from_pair, (k, k), h, pair_send.at[k, h], pair_recv.at[k, h], pair
+        )
+
     def to_middle(k, h):
-        return part_copy(k, from_end, k, h, end_send.at[k, h], end_recv.at[k, h], toward)
+        return part_copy(sums, from_end, (k, k), h, end_send.at[k, h], end_recv.at[k, h], toward)
 
     def across(k, h):
-        return part_copy(k, from_mid, k, h, mid_send.at[k, h], mid_recv.at[k, h], toward)
+        return part_copy(sums, from_mid, (k, k), h, mid_send.at[k, h], mid_recv.at[k, h], toward)
 
     def to_end(h):
-        return part_copy(3, from_mid, 0, h, back_send.at[h], mid_recv.at[0, h], behind)
-
-    pair_copies = []
-    for k in range(4):
-        copies[2 * k].wait()
-
-        @pl.loop(0, width // tile)
-        def _(j):
-            columns = pl.ds(pl.multiple_of(j * tile, tile), tile)
-            for_pair[k, :, columns] = jnp.dot(
-                heads_ref[...], weights[k, 0, :, columns], preferred_element_type=jnp.float32
+        return part_copy(sums, from_mid, (3, 0), h, back_send.at[h], mid_recv.at[0, h], behind)
+
+    for h in range(parts):
+        for k in range(4):
+            copies[h, k, 0].wait()
+            for_pair[k, :, cut(h)] = jnp.dot(
+                heads_ref[...], weights[k, 0, :, cut(h)], preferred_element_type=jnp.float32
             ).astype(jnp.bfloat16)
-
-        copy = pltpu.make_async_remote_copy(
-            src_ref=for_pair.at[k],
-            dst_ref=from_pair.at[k],
-            send_sem=pair_send.at[k],
-            recv_sem=pair_recv.at[k],
-            device_id={"mp": pair},
-            device_id_type=MESH,
-        )
-        copy.start()
-        pair_copies.append(copy)
-        copies[2 * k + 1].wait()
-        copy.wait_recv()
-
-        @pl.loop(0, width // tile)
-        def _(j):
-            columns = pl.ds(pl.multiple_of(j * tile, tile), tile)
+            to_pair(k, h).start()
+        for k in range(4):
+            copies[h, k, 1].wait()
             mixed = jnp.dot(
-                heads_ref[...], weights[k, 1, :, columns], preferred_element_type=jnp.float32
+                heads_ref[...], weights[k, 1, :, cut(h)], preferred_element_type=jnp.float32
             )
-            sums[k, :, columns] = (mixed + from_pair[k, :, columns].astype(jnp.float32)).astype(
+            to_pair(k, h).wait_recv()
+            sums[k, :, cut(h)] = (mixed + from_pair[k, :, cut(h)].astype(jnp.float32)).astype(
                 jnp.bfloat16
             )
-
-        if k < 3:
-
-            @pl.when(jnp.logical_not(middle))
+            if k < 3:
+
+                @pl.when(jnp.logical_not(middle))
+                def _():
+                    to_middle(k, h).start()
+
+    def add(k, h, landing, slot):
+        total = sums[k, :, cut(h)].astype(jnp.float32) + landing[slot, :, cut(h)].astype(jnp.float32)
+        sums[k, :, cut(h)] = total.astype(jnp.bfloat16)
+
+    def finish(h, k, landings):
+        total = sums[k, :, cut(h)].astype(jnp.float32)
+        for landing, slot in landings:
+            total = total + landing[slot, :, cut(h)].astype(jnp.float32)
+        out_ref[:, cut(h)] = (residual_ref[:, cut(h)].astype(jnp.float32) + total).astype(
+            jnp.bfloat16
+        )
+
+    def rim_copy(h):
+        return pltpu.make_async_remote_copy(
+            src_ref=out_ref.at[pl.ds(rows - pad, pad), cut(h)],
+            dst_ref=rim.at[:, cut(h)],
+            send_sem=rim_send.at[h],
+            recv_sem=rim_recv.at[h],
+            device_id={"ctx": lax.rem(segment + 1, n)},
+            device_id_type=MESH,
+        )
+
+    def state_copy(p, h):
+        return pltpu.make_async_remote_copy(
+            src_ref=state_out.at[:, cut(h)],
+            dst_ref=states_in.at[p, :, cut(h)],
+            send_sem=state_send.at[p, h],
+            recv_sem=state_recv.at[p, h],
+            device_id={"ctx": lax.rem(segment + p, n)},
+            device_id_type=MESH,
+        )
+
+    def groups_of(h):
+        return pl.loop(h * part // LANES, (h + 1) * part // LANES)
+
+    def lanes_of(g):
+        return pl.ds(pl.multiple_of(g * LANES, LANES), LANES)
+
+    def states_part(h):
+        @pl.when(segment > 0)
+        def _():
+            rim_copy(h).wait_recv()
+
+        @groups_of(h)
+        def _(g):
+            lanes = lanes_of(g)
+            make_signal(
+                out_ref.at[:, lanes], rim.at[:, lanes], gate_in_ref.at[:, lanes],
+                taps_ref.at[:, lanes], stream, signal.at[g],
+            )
+            recurrence_states(signal.at[g], rates_ref.at[:, lanes], ends.at[g], state_out.at[:, lanes])
+
+        for p in range(1, n):
+
+            @pl.when(segment + p < n)
             def _():
-                for h in range(parts):
-                    to_middle(k, h).start()
-
-    def add(k, h, landing, slot):
-        piece = pl.ds(h * part, part)
-        total = sums[k, piece, :].astype(jnp.float32) + landing[slot, piece, :].astype(jnp.float32)
-        sums[k, piece, :] = total.astype(jnp.bfloat16)
-
-    def finish(h, k, landings):
-        piece = pl.ds(h * part, part)
-        total = sums[k, piece, :].astype(jnp.float32)
-        for landing, slot in landings:
-            total = total + landing[slot, piece, :].astype(jnp.float32)
-        out_ref[piece, :] = (residual_ref[piece, :].astype(jnp.float32) + total).astype(jnp.bfloat16)
-
-    @pl.when(middle)
-    def _():
-        for k in range(2):
-            for h in range(parts):
+                state_copy(p, h).start()
+
+    def outputs_part(h):
+        for p in range(1, n):
+
+            @pl.when(segment >= p)
+            def _():
+                state_copy(p, h).wait_recv()
+
+        @groups_of(h)
+        def _(g):
+            lanes = lanes_of(g)
+            rates = rates_ref.at[:, lanes]
+            span = jnp.exp(-rates[...] * float(rows))
+            before = jnp.zeros((poles, LANES), jnp.float32)
+            for p in range(n - 1, 0, -1):
+                before = span * before + states_in[p, :, lanes]
+            recurrence_outputs(signal.at[g], rates, residues_ref.at[:, lanes], ends.at[g], before, conv)
+            mixed = conv[...] + skip_ref[:, lanes] * signal[g]
+            hyena_ref[:, lanes] = (gate_out_ref[:, lanes].astype(jnp.float32) * mixed).astype(
+                jnp.bfloat16
+            )
+
+    for h in range(parts):
+
+        @pl.when(middle)
+        def _():
+            for k in range(2):
                 to_middle(k, h).wait_recv()
                 add(k, h, from_end, k)
                 across(k, h).start()
-        for h in range(parts):
             across(0, h).wait_recv()
             add(3, h, from_mid, 0)
             to_end(h).start()
-        for h in range(parts):
             to_middle(2, h).wait_recv()
             across(1, h).wait_recv()
             finish(h, 2, ((from_end, 2), (from_mid, 1)))
-        for h in range(parts):
+
+        @pl.when(jnp.logical_not(middle))
+        def _():
+            across(0, h).wait_recv()
+            finish(h, 3, ((from_mid, 0),))
+
+        @pl.when(segment < n - 1)
+        def _():
+            rim_copy(h).start()
+
+        if h:
+            outputs_part(h - 1)
+        states_part(h)
+    outputs_part(parts - 1)
+
+    for h in range(parts):
+        for k in range(4):
+            to_pair(k, h).wait_send()
+
+        @pl.when(middle)
+        def _():
             across(0, h).wait_send()
             across(1, h).wait_send()
             to_end(h).wait_send()
 
-    @pl.when(jnp.logical_not(middle))
-    def _():
-        for h in range(parts):
-            across(0, h).wait_recv()
-            finish(h, 3, ((from_mid, 0),))
-        for k in range(3):
-            for h in range(parts):
+        @pl.when(jnp.logical_not(middle))
+        def _():
+            for k in range(3):
                 to_middle(k, h).wait_send()
 
-    for copy in pair_copies:
-        copy.wait_send()
-
-
-def project_reduce(heads_out, residual_in, out_weight):
+        @pl.when(segment < n - 1)
+        def _():
+            rim_copy(h).wait_send()
+
+        for p in range(1, n):
+
+            @pl.when(segment + p < n)
+            def _():
+                state_copy(p, h).wait_send()
+
+
+def project_hyena(
+    heads_out, residual_in, out_weight, gate_in, gate_out, short_taps, decay_rates, residues, skip_gain
+):
     rows, width = residual_in.shape
     depth = heads_out.shape[1]
-    parts = 4 if rows % 64 == 0 else 1
+    n = lax.axis_size("ctx")
+    poles = decay_rates.shape[0]
+    groups = width // LANES
+    parts = min(4, groups)
+    pad = 16
     vmem = pl.BlockSpec(memory_space=pltpu.VMEM)
     dma = pltpu.SemaphoreType.DMA
+    block = jax.ShapeDtypeStruct((rows, width), jnp.bfloat16)
 
     def blocks(count):
         return pltpu.VMEM((count, rows, width), jnp.bfloat16)
 
+    def floats(*dims):
+        return pltpu.VMEM(dims, jnp.float32)
+
     return pl.pallas_call(
-        project_reduce_kernel,
-        in_specs=[vmem, vmem, pl.BlockSpec(memory_space=pl.ANY)],
-        out_specs=vmem,
-        out_shape=jax.ShapeDtypeStruct((rows, width), jnp.bfloat16),
+        functools.partial(project_hyena_kernel, n),
+        in_specs=[vmem, vmem, pl.BlockSpec(memory_space=pl.ANY)] + [vmem] * 6,
+        out_specs=[vmem, vmem],
+        out_shape=[block, block],
         scratch_shapes=[
             pltpu.VMEM((4, 2, depth, width), jnp.bfloat16),
             blocks(4), blocks(4), blocks(4), blocks(3), blocks(2),
-            dma((4, 2)), dma((4,)), dma((4,)),
+            pltpu.VMEM((pad, width), jnp.bfloat16),
+            floats(pad + rows, LANES), floats(groups, rows, LANES), floats(rows, LANES),
+            floats(groups, CHUNKS, poles, LANES), floats(poles, width), floats(n, poles, width),
+            dma((parts, 4, 2)), dma((4, parts)), dma((4, parts)),
             dma((3, parts)), dma((3, parts)), dma((2, parts)), dma((2, parts)), dma((parts,)),
+            dma((parts,)), dma((parts,)), dma((n, parts)), dma((n, parts)),
         ],
         compiler_params=pltpu.CompilerParams(
-            collective_id=2, has_side_effects=True, vmem_limit_bytes=56 * 1024 * 1024
+            collective_id=2, has_side_effects=True, vmem_limit_bytes=58 * 1024 * 1024
         ),
         cost_estimate=pl.CostEstimate(
             flops=16 * rows * depth * width,
-            bytes_accessed=16 * depth * width + 6 * rows * width,
+            bytes_accessed=16 * depth * width + 12 * rows * width,
             transcendentals=0,
         ),
-    )(heads_out, residual_in, out_weight)
+    )(
+        heads_out, residual_in, out_weight, gate_in, gate_out, short_taps, decay_rates, residues,
+        skip_gain[None],
+    )
 
 
 def from_behind(value, axis, steps):
@@ -574,15 +689,19 @@
         heads_out = attend([(query_rows, query_pos)], key_rows, value_rows)[0]
         heads_out = heads_out.transpose(1, 0, 2).reshape(rows, width)
     if lax.axis_size("mp") == 8:
-        attended = project_reduce(heads_out, residual_in, out_weight)
-    else:
-        partial = jnp.einsum(
-            "qk,kc->cq", heads_out, out_weight, preferred_element_type=jnp.float32
-        ).astype(jnp.bfloat16)
-        projected = lax.psum_scatter(partial, "mp", scatter_dimension=0, tiled=True)
-        attended = (
-            residual_in.astype(jnp.float32) + projected.astype(jnp.float32).T
-        ).astype(jnp.bfloat16)
+        return tuple(
+            project_hyena(
+                heads_out, residual_in, out_weight, gate_in, gate_out, short_taps, decay_rates,
+                residues, skip_gain,
+            )
+        )
+    partial = jnp.einsum(
+        "qk,kc->cq", heads_out, out_weight, preferred_element_type=jnp.float32
+    ).astype(jnp.bfloat16)
+    projected = lax.psum_scatter(partial, "mp", scatter_dimension=0, tiled=True)
+    attended = (
+        residual_in.astype(jnp.float32) + projected.astype(jnp.float32).T
+    ).astype(jnp.bfloat16)
     hyena_out = hyena(attended, gate_in, gate_out, short_taps, decay_rates, residues, skip_gain)
     return (attended, hyena_out)
 

time: 180 us -> 161 us (0.89)
  blocking collectives: 13.6 us -> 0 us
  Pallas kernels: 153 us -> 149 us
    all_gather x1 -> x0, blocking collectives: 13.6 us -> none  [hyena(): states = lax.all_gather(state, 'ctx', axis=0)]
    pallas_call x3 -> x1, Pallas kernels: 102 us -> 98.1 us  [project_hyena(): pl.pallas_call(functools.partial(project_hyena_kernel, n), in_specs=[vmem...]
    unnamed x13 -> x10, local copies, waits for them, and re-layouts: 7.5 us -> 9.16 us
  transfers between devices with their start and end apart: 1 -> 0, of which waited for: 1 -> 0; matrix products, arithmetic and copies ran while one was open for 0% -> 0% of each run, Pallas kernels for 0% -> 0%
where the time goes in v3:
time: 161 us; the launch traced here: 158 us
  Pallas kernels  149 us (93%)
  local copies, waits for them, and re-layouts  9.16 us (6%)
    pallas_call x1, Pallas kernels, project_hyena(): pl.pallas_call(functools.partial(project_hyena_kernel, n), in_specs=[vmem...  98.1 us
    pallas_call x1, Pallas kernels, spread_attention(): pl.pallas_call(functools.partial(spread_attention_kernel, n, min(256, row...  50.5 us
    unnamed x10, local copies, waits for them, and re-layouts  9.16 us

profile of v3, /device:TPU:0, one launch (start us, length us, event | category | flops | bytes accessed | tf_op | source)
XLA Modules:
  0.0 158.4 jit_solution(7153228528054597412)
XLA Ops:
  0.6 0.0 copy-start
  0.6 1.2 copy-done
  1.9 0.0 copy-start.1
  1.9 1.2 copy-done.1
  3.1 0.0 copy-start.2
  3.1 1.2 copy-done.2
  4.3 50.5 %shard_map.122.heads_ref = bf16[512,1024]{1,0:T(8,128)(2,1)S(1)} custom-call(bf16[512,1024]{1,0:T(8,128)(2,1)S(1)} %copy-done, bf16[512,1024]{1,0:T(8,128)(2,1)S(1)} %copy-done.1, bf16[512,1024]{1,0:T(8,128)(2,1)S(1)} %copy-done.2), custom_call_target="tpu_custom_call" | custom-call | flops 2147483648 | bytes 4194304 | tf_op jit(solution)/shard_map/pallas_call | solution.py:155
  54.8 0.0 copy-start.3
  54.8 1.0 copy-done.3
  55.8 98.1 %shard_map.123 = (bf16[512,1024]{1,0:T(8,128)(2,1)}, bf16[512,1024]{1,0:T(8,128)(2,1)}) custom-call(bf16[512,1024]{1,0:T(8,128)(2,1)} %copy-done.3, bf16[512,1024]{1,0:T(8,128)(2,1)} %residual_ref.1, bf16[1024,8192]{1,0:T(8,128)(2,1)} %weight_ref.1, bf16[512,1024]{1,0:T(8,128)(2,1)} %gate_in_ref.1, bf16[512,1024]{1,0:T(8,128)(2,1)} %gate_out_ref.1, ...), custom_call_target="tpu_custom_call" | custom-call | flops 8589934592 | bytes 23068672 | tf_op jit(solution)/shard_map/pallas_call | solution.py:444
  153.9 2.3 %copy.15 = bf16[512,1024]{1,0:T(8,128)(2,1)} copy(bf16[512,1024]{1,0:T(8,128)(2,1)} %get-tuple-element.4) | data formatting | bytes 2097152
  156.2 2.3 %copy.16 = bf16[512,1024]{1,0:T(8,128)(2,1)} copy(bf16[512,1024]{1,0:T(8,128)(2,1)} %get-tuple-element.5) | data formatting | bytes 2097152
Async XLA Ops:
  0.6 1.2 copy-start
  1.9 1.2 copy-start.1
  3.1 1.2 copy-start.2
  54.8 1.0 copy-start.3

commit v4 on v3

--- a/solution.py
+++ b/solution.py
@@ -163,7 +163,7 @@
             dma((heads, n)), dma((heads, n)), dma((heads,)),
         ],
         compiler_params=pltpu.CompilerParams(
-            collective_id=1, has_side_effects=True, vmem_limit_bytes=48 * 1024 * 1024
+            collective_id=1, has_side_effects=True, vmem_limit_bytes=60 * 1024 * 1024
         ),
         cost_estimate=pl.CostEstimate(
             flops=2 * length * length * heads * HD,

time: 161 us -> 156 us (0.969)
  local copies, waits for them, and re-layouts: 9.16 us -> 4.52 us
    unnamed x10 -> x2, local copies, waits for them, and re-layouts: 9.16 us -> 4.52 us
where the time goes in v4:
time: 156 us; the launch traced here: 154 us
  Pallas kernels  149 us (96%)
  local copies, waits for them, and re-layouts  4.52 us (3%)
    pallas_call x1, Pallas kernels, project_hyena(): pl.pallas_call(functools.partial(project_hyena_kernel, n), in_specs=[vmem...  98.2 us
    pallas_call x1, Pallas kernels, spread_attention(): pl.pallas_call(functools.partial(spread_attention_kernel, n, min(256, row...  50.8 us
    unnamed x2, local copies, waits for them, and re-layouts  4.52 us

profile of v4, /device:TPU:0, one launch (start us, length us, event | category | flops | bytes accessed | tf_op | source)
XLA Modules:
  0.0 154.1 jit_solution(2962763090057188142)
XLA Ops:
  0.6 50.8 %shard_map.122.heads_ref = bf16[512,1024]{1,0:T(8,128)(2,1)} custom-call(bf16[512,1024]{1,0:T(8,128)(2,1)} %query_ref.1, bf16[512,1024]{1,0:T(8,128)(2,1)} %key_ref.1, bf16[512,1024]{1,0:T(8,128)(2,1)} %value_ref.1), custom_call_target="tpu_custom_call" | custom-call | flops 2147483648 | bytes 4194304 | tf_op jit(solution)/shard_map/pallas_call | solution.py:155
  51.4 98.2 %shard_map.123 = (bf16[512,1024]{1,0:T(8,128)(2,1)}, bf16[512,1024]{1,0:T(8,128)(2,1)}) custom-call(bf16[512,1024]{1,0:T(8,128)(2,1)} %shard_map.122.heads_ref, bf16[512,1024]{1,0:T(8,128)(2,1)} %residual_ref.1, bf16[1024,8192]{1,0:T(8,128)(2,1)} %weight_ref.1, bf16[512,1024]{1,0:T(8,128)(2,1)} %gate_in_ref.1, bf16[512,1024]{1,0:T(8,128)(2,1)} %gate_out_ref.1, ...), custom_call_target="tpu_custom_call" | custom-call | flops 8589934592 | bytes 23068672 | tf_op jit(solution)/shard_map/pallas_call | solution.py:444
  149.6 2.3 %copy.15 = bf16[512,1024]{1,0:T(8,128)(2,1)} copy(bf16[512,1024]{1,0:T(8,128)(2,1)} %get-tuple-element.4) | data formatting | bytes 2097152
  151.9 2.3 %copy.16 = bf16[512,1024]{1,0:T(8,128)(2,1)} copy(bf16[512,1024]{1,0:T(8,128)(2,1)} %get-tuple-element.5) | data formatting | bytes 2097152
